TPU v7x, 32 devices: a whole 2x2x4 slice. The times are simulated.
32 devices in a mesh: tile: 16 (over z, y, core), layer: 2 (over x).
Axes of the slice: x: 2, y: 2, z: 4, core: 2. Of those that a mesh axis runs over, the one named last changes fastest.
Arguments:
- warmth_level: float32 [16, 16, 512], P('layer', 'tile'), may hold values from -6 to 6
- heat_flow_ability: float32 [16, 16, 512], P('layer', 'tile'), may hold values from 0.5 to 2
- material_zone_label: int32 [16, 16, 512], P('layer', 'tile'), may hold values from 0 to 3
- reciprocal_warming_storage: float32 [4], replicated, may hold values from 0.5 to 2
- collector_potential_field: float32 [16, 16, 512], P('layer', 'tile'), may hold values from -4 to 4
- tab_indicator: int32 [16, 512], P('tile'), may hold values 0 or 1
- sheet_node_link_matrix: float32 [40, 16], replicated, may hold values from -1.5 to 1.5
- solution_salt_level: float32 [40, 16, 512], P(None, 'tile', 'layer'), may hold values from -6 to 6
- grain_shell_level: float32 [32, 40, 16, 512], P(None, None, 'tile', 'layer'), may hold values from -6 to 6
- solution_diffusion_matrix: float32 [40, 40], replicated, may hold values from -1 to 1.5
- grain_diffusion_matrix: float32 [32, 32], replicated, may hold values from -1 to 1.5
Outputs:
- next_warmth_level: float32 [16, 16, 512], P('layer', 'tile')
- reaction_warming_sheets: float32 [16, 16, 512], P('layer', 'tile')
- reaction_flux_sheets: float32 [16, 16, 512], P('layer', 'tile')
- next_grain_level: float32 [32, 40, 16, 512], P(None, None, 'tile', 'layer')
- next_solution_level: float32 [40, 16, 512], P(None, 'tile', 'layer')
All inputs are finite; a program needn't handle non-finite values. No bound on the sum of `tab_indicator` on one device may be relied on, other than what follows from the above.
Results may differ from a plain program's by a relative error of at most 0.0002.
Values sent between devices are 32-bit elements; how exact they have to be, the bound alone decides.
No kernel may reach another device: no remote copies, remote signals or barrier semaphores. Data moves between devices by JAX's collectives and lax.ppermute only.
A program may use at most 64 MiB of HBM per device.

v0:
```python
import functools

import jax
import jax.numpy as jnp
from jax import lax
from jax.experimental import pallas as pl
from jax.experimental.pallas import tpu as pltpu
from jax.sharding import PartitionSpec as P

SWEEPS = 3
BV_ITERS = 4


warming_advance = 0.04
damping_weight = 4.5
imposed_excitation = 0.6
shell_flux = 0.5
film_resist = 0.5

LANES = 128
ROWS = 8
LOG2 = 0.6931471805599453
HIGHEST = lax.Precision.HIGHEST


def extended(block, sides, width):
    for axis, dim in sides:
        count = lax.axis_size(axis)
        forward = [(i, i + 1) for i in range(count - 1)]
        backward = [(target, source) for source, target in forward]
        low = lax.ppermute(
            lax.slice_in_dim(block, block.shape[dim] - width, None, axis=dim), axis, forward
        )
        high = lax.ppermute(lax.slice_in_dim(block, 0, width, axis=dim), axis, backward)
        block = jnp.concatenate([low, block, high], axis=dim)
    return block


def advance_stack_vertical(
    temp_col,
    volt_col,
    sheet_node_link_matrix,
    solution_salt_level,
    grain_shell_level,
    solution_diffusion_matrix,
    grain_diffusion_matrix,
):
    highest = lax.Precision.HIGHEST
    shells = grain_diffusion_matrix.shape[0]
    node_temp = jnp.einsum("el,lxy->exy", sheet_node_link_matrix, temp_col, precision=highest)
    node_voltage = jnp.einsum("el,lxy->exy", sheet_node_link_matrix, volt_col, precision=highest)
    next_solution_level = jnp.einsum(
        "ef,fxy->exy", solution_diffusion_matrix, solution_salt_level, precision=highest
    )
    surface_base = jnp.einsum(
        "s,sexy->exy", grain_diffusion_matrix[shells - 1], grain_shell_level, precision=highest
    )
    gain = shell_flux * grain_diffusion_matrix[shells - 1, shells - 1]
    rate = 0.5 * jax.nn.sigmoid(0.3 * node_temp) * jax.nn.sigmoid(next_solution_level)
    reaction = jnp.zeros_like(node_temp)
    for iteration in range(BV_ITERS):
        surface = surface_base - gain * reaction
        overvoltage = node_voltage - jnp.tanh(surface) - film_resist * reaction
        reaction = 2.0 * rate * jnp.sinh(0.5 * overvoltage)
    surface = surface_base - gain * reaction
    source = reaction * (node_voltage - jnp.tanh(surface))
    next_grain_level = jnp.einsum(
        "st,texy->sexy", grain_diffusion_matrix, grain_shell_level, precision=highest
    )
    next_grain_level = (
        next_grain_level
        - shell_flux * grain_diffusion_matrix[:, shells - 1][:, None, None, None] * reaction[None]
    )
    reaction_warming_sheets = jnp.einsum(
        "el,exy->lxy", sheet_node_link_matrix, source, precision=highest
    )
    reaction_flux_sheets = jnp.einsum(
        "el,exy->lxy", sheet_node_link_matrix, reaction, precision=highest
    )
    return (reaction_warming_sheets, reaction_flux_sheets, next_grain_level, next_solution_level)


def four_border_faces(bordered_lattice):
    return (
        bordered_lattice[:, 2:, 1:-1]
        + bordered_lattice[:, :-2, 1:-1]
        + bordered_lattice[:, 1:-1, 2:]
        + bordered_lattice[:, 1:-1, :-2]
    )


def per_device_general(
    warmth_level,
    heat_flow_ability,
    material_zone_label,
    reciprocal_warming_storage,
    collector_potential_field,
    tab_indicator,
    sheet_node_link_matrix,
    solution_salt_level,
    grain_shell_level,
    solution_diffusion_matrix,
    grain_diffusion_matrix,
):
    stored_coulomb_limit = jnp.zeros_like(warmth_level)
    for label in range(reciprocal_warming_storage.shape[0]):
        stored_coulomb_limit = stored_coulomb_limit + jnp.where(
            material_zone_label == label, reciprocal_warming_storage[label], 0.0
        )
    bordered_lattice = extended(warmth_level, (("tile", 1), ("layer", 0)), 1)
    bordered_lattice = jnp.pad(bordered_lattice, ((0, 0), (0, 0), (1, 1)))
    neighbour_entries = bordered_lattice[2:, 1:-1, 1:-1] + bordered_lattice[:-2, 1:-1, 1:-1]
    neighbour_entries = (
        neighbour_entries + bordered_lattice[1:-1, 2:, 1:-1] + bordered_lattice[1:-1, :-2, 1:-1]
    )
    neighbour_entries = (
        neighbour_entries + bordered_lattice[1:-1, 1:-1, 2:] + bordered_lattice[1:-1, 1:-1, :-2]
    )
    next_warmth_level = (
        warmth_level
        + warming_advance
        * stored_coulomb_limit
        * heat_flow_ability
        * (neighbour_entries - 6.0 * warmth_level)
    )
    bounded_entries = (1 - tab_indicator).astype(jnp.float32)[None]
    battery_potential_drop = collector_potential_field
    for sweep in range(SWEEPS):
        enclosed_lattice = extended(battery_potential_drop, (("tile", 1),), 1)
        enclosed_lattice = jnp.pad(enclosed_lattice, ((0, 0), (0, 0), (1, 1)))
        battery_potential_drop = (
            bounded_entries
            * (four_border_faces(enclosed_lattice) + imposed_excitation * next_warmth_level)
            / damping_weight
        )
    temp_col, volt_col = (
        lax.all_to_all(next_warmth_level, "layer", split_axis=2, concat_axis=0, tiled=True),
        lax.all_to_all(battery_potential_drop, "layer", split_axis=2, concat_axis=0, tiled=True),
    )
    heat_col, current_col, next_grain_level, next_solution_level = advance_stack_vertical(
        temp_col,
        volt_col,
        sheet_node_link_matrix,
        solution_salt_level,
        grain_shell_level,
        solution_diffusion_matrix,
        grain_diffusion_matrix,
    )
    reaction_warming_sheets, reaction_flux_sheets = (
        lax.all_to_all(heat_col, "layer", split_axis=0, concat_axis=2, tiled=True),
        lax.all_to_all(current_col, "layer", split_axis=0, concat_axis=2, tiled=True),
    )
    return (
        next_warmth_level,
        reaction_warming_sheets,
        reaction_flux_sheets,
        next_grain_level,
        next_solution_level,
    )


def along_span(field, blocks):
    rows = field.shape[0]
    lane = lax.broadcasted_iota(jnp.int32, field.shape, 1)
    block = lax.rem(lax.broadcasted_iota(jnp.int32, field.shape, 0), blocks)
    low = pltpu.roll(field, 1, 1)
    low_carry = jnp.where(block == 0, 0.0, pltpu.roll(low, 1, 0))
    high = pltpu.roll(field, LANES - 1, 1)
    high_carry = jnp.where(block == blocks - 1, 0.0, pltpu.roll(high, rows - 1, 0))
    return jnp.where(lane == 0, low_carry, low) + jnp.where(lane == LANES - 1, high_carry, high)


def along_sheets(field, blocks):
    rows = field.shape[0]
    row = lax.broadcasted_iota(jnp.int32, field.shape, 0)
    low = jnp.where(row < blocks, 0.0, pltpu.roll(field, blocks, 0))
    high = jnp.where(row >= rows - blocks, 0.0, pltpu.roll(field, rows - blocks, 0))
    return low + high


def fetch(pairs, sems):
    copies = [pltpu.make_async_copy(src, dst, sems.at[i]) for i, (src, dst) in enumerate(pairs)]
    for copy in copies:
        copy.start()
    return copies


def pack_kernel(
    blocks, storage, warmth, ability, zone, potential, tab, out, regions, heat, label, tabs, sems
):
    n = warmth.shape[0]
    copies = fetch(
        (
            (storage, regions),
            (zone, label),
            (ability, heat),
            (tab, tabs),
            (warmth, out.at[0:n]),
            (potential, out.at[n : 2 * n]),
        ),
        sems,
    )
    for copy in copies[:4]:
        copy.wait()
    zones = label[...]
    capacity = jnp.full(zones.shape, regions[0])
    for region in range(1, regions.shape[0]):
        capacity = jnp.where(zones == region, regions[region], capacity)
    out[2 * n : 3 * n, :] = warming_advance * capacity * heat[...]
    free = (1 - tabs[...]).astype(jnp.float32) * (1.0 / damping_weight)
    out[3 * n : 3 * n + blocks, :] = free
    out[3 * n + blocks : 3 * n + 2 * blocks, :] = free
    for copy in copies[4:]:
        copy.wait()


def spread(count, total, per):
    row = lax.broadcasted_iota(jnp.int32, (total, count), 0)
    column = lax.broadcasted_iota(jnp.int32, (total, count), 1)
    return (row // per == column).astype(jnp.float32)


def wide(matrix, per):
    rows, columns = matrix.shape
    left = spread(rows, rows * per, per)
    right = spread(columns, columns * per, per)
    full = jnp.dot(left, matrix, precision=HIGHEST, preferred_element_type=jnp.float32)
    full = lax.dot_general(
        full, right, (((1,), (1,)), ((), ())), precision=HIGHEST, preferred_element_type=jnp.float32
    )
    row = lax.broadcasted_iota(jnp.int32, full.shape, 0)
    column = lax.broadcasted_iota(jnp.int32, full.shape, 1)
    return jnp.where(lax.rem(row, per) == lax.rem(column, per), full, 0.0)


def halves(value):
    high = value.astype(jnp.bfloat16)
    return high, (value - high.astype(jnp.float32)).astype(jnp.bfloat16)


def local_kernel(
    diffusion, grain, salt, salt_matrix, held, local, weights, level, matrix, sems, grain_sems
):
    shells, nodes, _ = grain.shape
    part = shells // grain_sems.shape[0]
    small = fetch(((salt, level), (salt_matrix, matrix), (diffusion, weights)), sems)
    copies = fetch(
        [
            (grain.at[s : s + part], held.at[s : s + part])
            for s in range(0, shells, part)
        ],
        grain_sems,
    )
    for copy in small:
        copy.wait()
    local[nodes : 2 * nodes, :] = jnp.dot(
        wide(matrix[...], nodes // matrix.shape[0]),
        level[...],
        precision=HIGHEST,
        preferred_element_type=jnp.float32,
    )
    surface = jnp.zeros((nodes, LANES), jnp.float32)
    for i, copy in enumerate(copies):
        copy.wait()
        for shell in range(i * part, (i + 1) * part):
            surface = surface + weights[shells - 1, shell] * held[shell]
    local[0:nodes, :] = surface


def grain_kernel(grain, shells_matrix, base):
    shells, nodes, _ = grain.shape
    matrix_high, matrix_low = halves(wide(shells_matrix[...], ROWS))
    for start in range(0, nodes, 2 * ROWS):
        pair = [
            grain[:, start + k * ROWS : start + (k + 1) * ROWS, :].reshape(shells * ROWS, LANES)
            for k in range(2)
        ]
        high, low = halves(jnp.concatenate(pair, axis=1))
        dot = functools.partial(jnp.dot, preferred_element_type=jnp.float32)
        result = dot(matrix_high, high) + (dot(matrix_high, low) + dot(matrix_low, high))
        for k in range(2):
            part = result[:, k * LANES : (k + 1) * LANES].reshape(shells, ROWS, LANES)
            base[:, start + k * ROWS : start + (k + 1) * ROWS, :] = part


def sweep_kernel(sheets, blocks, tiles, local, own, partner, near, far, inner, out, masks):
    n = sheets * blocks
    size = own.shape[0]
    tile = lax.axis_index("tile")
    block = lax.axis_index("layer")
    first = jnp.logical_or(tile == 0, tile == tiles - 1)
    second = jnp.logical_or(tile == 2, tile == tiles - 3)
    beside = jnp.logical_or(tile == 1, tile == tiles - 2)
    keep_outer = jnp.where(first, 0.0, 1.0)
    keep_far = jnp.where(jnp.logical_or(first, second), 0.0, 1.0)
    keep_inner = jnp.where(beside, 0.0, 1.0)

    def load(ref, start, rows, keep=None):
        value = ref[start : start + rows, :]
        return value if keep is None else keep * value

    def window(start, rows):
        return [
            load(near, size + start, rows, keep_outer),
            load(near, start, rows, keep_outer),
            load(own, start, rows),
            load(partner, start, rows),
            load(inner, start, rows, keep_inner),
        ]

    warmth = [load(far, 0, n, keep_far)] + window(0, n) + [load(inner, size, n, keep_inner)]
    volt = [load(far, n, n, keep_far)] + window(n, n) + [load(inner, size + n, n, keep_inner)]
    slope = window(2 * n, n)
    free = window(3 * n, 2 * blocks)
    for i in range(5):
        masks[2 * i * blocks : 2 * (i + 1) * blocks, :] = free[i]
    free = [jnp.concatenate([m] * (n // m.shape[0]), axis=0) for m in free]
    temp = []
    for i in range(5):
        w = warmth[i + 1]
        around = warmth[i] + warmth[i + 2] + along_sheets(w, blocks) + along_span(w, blocks)
        temp.append(w + slope[i] * (around - 6.0 * w))
    for sweep in range(SWEEPS):
        volt = [
            free[i + sweep]
            * (
                volt[i]
                + volt[i + 2]
                + along_span(volt[i + 1], blocks)
                + imposed_excitation * temp[i + sweep]
            )
            for i in range(len(volt) - 2)
        ]
    out[0:n, :] = temp[2]
    out[n : 2 * n, :] = volt[0]
    for i in range(5):
        for k, value in enumerate((warmth[i + 1], slope[i])):
            edge = jnp.where(block == 0, value[n - blocks :, :], value[0:blocks, :])
            start = 2 * n + (2 * i + k) * blocks
            out[start : start + blocks, :] = edge
    out[2 * n + 10 * blocks :, :] = local[...]


def react(surface_base, gain, rate, node_voltage):
    reaction = jnp.zeros_like(node_voltage)
    for iteration in range(BV_ITERS):
        surface = surface_base - gain * reaction
        half = 0.5 * (node_voltage - jnp.tanh(surface) - film_resist * reaction)
        reaction = rate * (jnp.exp(half - LOG2) - jnp.exp(-half - LOG2))
    surface = surface_base - gain * reaction
    return reaction, reaction * (node_voltage - jnp.tanh(surface))


def reaction_kernel(
    sheets,
    blocks,
    diffusion,
    mine,
    other,
    masks,
    base,
    link,
    turned,
    next_warmth,
    warming,
    flux,
    grain_out,
    salt_out,
    weights,
    both,
    sheets_now,
    copy_out,
    sems,
    grain_sems,
):
    n = sheets * blocks
    shells, nodes, _ = base.shape
    block = lax.axis_index("layer")
    edge = 2 * blocks
    start = 2 * n + 5 * edge
    early = fetch(((diffusion, weights), (mine.at[start + nodes : start + 2 * nodes], salt_out)), sems)

    free = [masks[i * edge : (i + 1) * edge, :] for i in range(5)]
    added = []
    for i in range(5):
        at = 2 * n + i * edge
        added.append(pltpu.roll(mine[at : at + edge, :], blocks, 0) * other[at : at + edge, :])
    volt = [jnp.zeros_like(added[0])] * 7
    for sweep in range(SWEEPS):
        volt = [
            free[i + sweep]
            * (
                volt[i]
                + volt[i + 2]
                + along_span(volt[i + 1], blocks)
                + imposed_excitation * added[i + sweep]
            )
            for i in range(len(volt) - 2)
        ]
    here = pl.ds(pl.multiple_of(block * n, ROWS), n)
    there = pl.ds(pl.multiple_of((1 - block) * n, ROWS), n)
    both[here, 0:LANES] = mine[0:n, :]
    both[there, 0:LANES] = other[0:n, :]
    both[here, LANES:] = mine[n : 2 * n, :]
    both[there, LANES:] = other[n : 2 * n, :]
    extra = jnp.concatenate([added[2], volt[0]], axis=1)
    extra = jnp.where(block == 0, extra, pltpu.roll(extra, blocks, 0))
    both[n - blocks : n + blocks, :] += extra
    warmth_copy = pltpu.make_async_copy(both.at[here, 0:LANES], next_warmth, sems.at[2])
    warmth_copy.start()

    dot = functools.partial(jnp.dot, precision=HIGHEST, preferred_element_type=jnp.float32)
    node = dot(link[...], both[...])
    early[0].wait()
    gain = shell_flux * weights[shells - 1, shells - 1]
    results = []
    for part, ref in enumerate((mine, other)):
        rows = slice(part * nodes, (part + 1) * nodes)
        node_temp, node_voltage = node[rows, 0:LANES], node[rows, LANES:]
        surface_base = ref[start : start + nodes, :]
        salt = ref[start + nodes : start + 2 * nodes, :]
        rate = 1.0 / ((1.0 + jnp.exp(-0.3 * node_temp)) * (1.0 + jnp.exp(-salt)))
        results.append(react(surface_base, gain, rate, node_voltage))
        if part == 0:
            reaction = results[0][0]
            copies = []
            step = shells // grain_sems.shape[0]
            for first in range(0, shells, step):
                for shell in range(first, first + step):
                    factor = shell_flux * weights[shell, shells - 1]
                    copy_out[shell] = base[shell] - factor * reaction
                copies.append(
                    pltpu.make_async_copy(
                        copy_out.at[first : first + step],
                        grain_out.at[first : first + step],
                        grain_sems.at[first // step],
                    )
                )
                copies[-1].start()
    columns = jnp.concatenate([jnp.concatenate(r[::-1], axis=1) for r in results], axis=0)
    sheets_now[...] = dot(turned[...], columns)
    late = [
        pltpu.make_async_copy(sheets_now.at[:, 0:LANES], warming, sems.at[3]),
        pltpu.make_async_copy(sheets_now.at[:, LANES:], flux, sems.at[4]),
    ]
    for copy in late:
        copy.start()
    for copy in early[1:] + [warmth_copy] + copies + late:
        copy.wait()


def link_kernel(blocks, parts, link, turned, wide_link, wide_turned):
    nodes, sheets = link.shape
    per = blocks // parts
    own = sheets // parts
    rows, columns = nodes * blocks, sheets * blocks
    layer = lax.axis_index("layer")
    dot = functools.partial(jnp.dot, precision=HIGHEST, preferred_element_type=jnp.float32)

    def iota(shape):
        return [lax.broadcasted_iota(jnp.int32, shape, axis) for axis in range(2)]

    def fits(r, c):
        part = lax.rem(r // (nodes * per) + layer, parts)
        return lax.rem(c, blocks) == part * per + lax.rem(r, per)

    r, c = iota((rows, nodes))
    pick = (lax.rem(r, nodes * per) // per == c).astype(jnp.float32)
    r, c = iota((sheets, columns))
    split = (c // blocks == r).astype(jnp.float32)
    r, c = iota((rows, columns))
    wide_link[...] = jnp.where(fits(r, c), dot(dot(pick, link[...]), split), 0.0)
    r, c = iota((nodes, rows))
    pick = (lax.rem(c, nodes * per) // per == r).astype(jnp.float32)
    r, c = iota((own * blocks, sheets))
    split = (r // blocks + own * layer == c).astype(jnp.float32)
    r, c = iota((own * blocks, rows))
    wide_turned[...] = jnp.where(fits(c, r), dot(dot(split, turned[...]), pick), 0.0)


VMEM = pl.BlockSpec(memory_space=pltpu.VMEM)
SMEM = pl.BlockSpec(memory_space=pltpu.SMEM)
HBM = pl.BlockSpec(memory_space=pltpu.HBM)


def in_hbm(*values):
    return [pltpu.with_memory_space_constraint(value, pltpu.HBM) for value in values]


def shaped(*shape):
    return jax.ShapeDtypeStruct(shape, jnp.float32)


def call(kernel, name, out, ins, outs, flops, nbytes, scratch=()):
    return pl.pallas_call(
        kernel,
        out_shape=out,
        in_specs=ins,
        out_specs=outs,
        scratch_shapes=scratch,
        compiler_params=pltpu.CompilerParams(vmem_limit_bytes=32 * 1024 * 1024),
        cost_estimate=pl.CostEstimate(flops=flops, bytes_accessed=nbytes, transcendentals=0),
        name=name,
    )


def per_device(
    tiles,
    warmth_level,
    heat_flow_ability,
    material_zone_label,
    reciprocal_warming_storage,
    collector_potential_field,
    tab_indicator,
    sheet_node_link_matrix,
    solution_salt_level,
    grain_shell_level,
    solution_diffusion_matrix,
    grain_diffusion_matrix,
):
    sheets, _, span = warmth_level.shape
    shells, points, _, part = grain_shell_level.shape
    blocks = span // LANES
    nodes = points * part // LANES
    n = sheets * blocks
    edge = 2 * blocks

    def both_layers(pairs):
        return [(s * 2 + j, t * 2 + j) for s, t in pairs for j in range(2)]

    def across(where):
        return [(t * 2 + j, t * 2 + 1 - j) for t in where for j in range(2)]

    def mutual(pairs):
        return pairs + [(t, s) for s, t in pairs]

    def send(value, pairs):
        return lax.ppermute(value, ("tile", "layer"), pairs)

    cores = both_layers(mutual([(t, t + 1) for t in range(0, tiles, 2)]))
    beside = both_layers(mutual([(t, t - 1) for t in range(2, tiles, 2)]))
    beside = beside + across([0, tiles - 1])
    beyond = both_layers(mutual([(t, t - 3) for t in range(4, tiles, 2)]))
    beyond = beyond + across([0, 2, tiles - 3, tiles - 1])
    layers = across(range(tiles))

    own = call(
        functools.partial(pack_kernel, blocks),
        "pack",
        shaped(3 * n + edge, LANES),
        [HBM] * 6,
        VMEM,
        1000,
        100000,
        (
            pltpu.SMEM(reciprocal_warming_storage.shape, jnp.float32),
            pltpu.VMEM((n, LANES), jnp.float32),
            pltpu.VMEM((n, LANES), jnp.int32),
            pltpu.VMEM((blocks, LANES), jnp.int32),
            pltpu.SemaphoreType.DMA((6,)),
        ),
    )(
        *in_hbm(
            reciprocal_warming_storage,
            warmth_level.reshape(n, LANES),
            heat_flow_ability.reshape(n, LANES),
            material_zone_label.reshape(n, LANES),
            collector_potential_field.reshape(n, LANES),
            tab_indicator.reshape(blocks, LANES),
        )
    )
    partner = send(own, cores)
    near = send(jnp.concatenate([own, partner], axis=0), beside)
    far = send(own[0 : 2 * n], beyond)
    held, local = call(
        local_kernel,
        "columns",
        (shaped(shells, nodes, LANES), shaped(2 * nodes, LANES)),
        [HBM] * 4,
        (VMEM, VMEM),
        10**7,
        3000000,
        (
            pltpu.SMEM(grain_diffusion_matrix.shape, jnp.float32),
            pltpu.VMEM((nodes, LANES), jnp.float32),
            pltpu.VMEM(solution_diffusion_matrix.shape, jnp.float32),
            pltpu.SemaphoreType.DMA((3,)),
            pltpu.SemaphoreType.DMA((4,)),
        ),
    )(
        *in_hbm(
            grain_diffusion_matrix,
            grain_shell_level.reshape(shells, nodes, LANES),
            solution_salt_level.reshape(nodes, LANES),
            solution_diffusion_matrix,
        )
    )
    near, far, held, local = lax.optimization_barrier((near, far, held, local))
    inner = send(near, cores)
    mine, masks = call(
        functools.partial(sweep_kernel, sheets, blocks, tiles),
        "sweeps",
        (shaped(2 * n + 5 * edge + 2 * nodes, LANES), shaped(5 * edge, LANES)),
        [VMEM] * 6,
        (VMEM, VMEM),
        10**6,
        500000,
    )(local, own, partner, near, far, inner)
    other = send(mine, layers)
    held, masks = lax.optimization_barrier((held, masks))
    base = call(
        grain_kernel,
        "grains",
        shaped(shells, nodes, LANES),
        [VMEM] * 2,
        VMEM,
        10**9,
        3000000,
    )(held, grain_diffusion_matrix)
    link, turned = call(
        functools.partial(link_kernel, blocks, 2),
        "links",
        (shaped(points * blocks, 2 * n), shaped(n, points * blocks)),
        [VMEM] * 2,
        (VMEM, VMEM),
        10**7,
        100000,
    )(sheet_node_link_matrix, sheet_node_link_matrix.T)
    next_warmth, warming, flux, grain, salt = call(
        functools.partial(reaction_kernel, sheets, blocks),
        "reaction",
        (
            shaped(n, LANES),
            shaped(n, LANES),
            shaped(n, LANES),
            shaped(shells, nodes, LANES),
            shaped(nodes, LANES),
        ),
        [HBM] + [VMEM] * 6,
        (HBM,) * 5,
        10**7,
        3000000,
        (
            pltpu.SMEM(grain_diffusion_matrix.shape, jnp.float32),
            pltpu.VMEM((2 * n, 2 * LANES), jnp.float32),
            pltpu.VMEM((n, 2 * LANES), jnp.float32),
            pltpu.VMEM((shells, nodes, LANES), jnp.float32),
            pltpu.SemaphoreType.DMA((5,)),
            pltpu.SemaphoreType.DMA((4,)),
        ),
    )(*in_hbm(grain_diffusion_matrix), mine, other, masks, base, link, turned)
    return (
        next_warmth.reshape(warmth_level.shape),
        warming.reshape(warmth_level.shape),
        flux.reshape(warmth_level.shape),
        grain.reshape(grain_shell_level.shape),
        salt.reshape(solution_salt_level.shape),
    )


def solution(mesh):
    placed = (
        P("layer", "tile", None),
        P("layer", "tile", None),
        P("layer", "tile", None),
        P(),
        P("layer", "tile", None),
        P("tile", None),
        P(),
        P(None, "tile", "layer"),
        P(None, None, "tile", "layer"),
        P(),
        P(),
    )
    tiles, parts = mesh.shape["tile"], mesh.shape["layer"]
    plan = functools.partial(per_device, tiles) if parts == 2 else per_device_general
    return jax.shard_map(
        plan,
        mesh=mesh,
        in_specs=placed,
        out_specs=(
            P("layer", "tile", None),
            P("layer", "tile", None),
            P("layer", "tile", None),
            P(None, None, "tile", "layer"),
            P(None, "tile", "layer"),
        ),
        check_vma=False,
    )
```

profile of v0, /device:TPU:0, one launch (start us, length us, event | category | flops | bytes accessed | tf_op | source)
XLA Modules:
  0.0 19.5 jit_solution(10884460051340831122)
XLA Ops:
  0.6 0.0 copy-start
  0.6 0.0 copy-start.1
  0.7 0.9 %pack.1.own = f32[104,128]{1,0:T(8,128)S(1)} custom-call(f32[4]{0:T(128)} %storage.1, f32[32,128]{1,0:T(8,128)} %bitcast.16, f32[32,128]{1,0:T(8,128)} %bitcast.17, s32[32,128]{1,0:T(8,128)} %bitcast.18, f32[32,128]{1,0:T(8,128)} %bitcast.19, s32[4,128]{1,0:T(4,128)} %bitcast.20), custom_call_target="tpu_custom_call" | custom-call | flops 1000 | bytes 100000 | tf_op jit(solution)/shard_map/pack/pallas_call | solution.py:547
  1.5 0.5 %collective-permute-start = (f32[104,128]{1,0:T(8,128)S(1)}, f32[104,128]{1,0:T(8,128)S(1)}, u32[]{:S(2)}, u32[]{:S(2)}) collective-permute-start(f32[104,128]{1,0:T(8,128)S(1)} %pack.1.own), channel_id=1, source_target_pairs={{0,2},{1,3},{4,6},{5,7},{8,10},{9,11},{12,14},{13,15},{16,18},{17,... | collective-permute-start | bytes 159752 | tf_op jit(solution)/shard_map/ppermute | solution.py:538
  2.0 0.9 %collective-permute-done.partner = f32[104,128]{1,0:T(8,128)S(1)} collective-permute-done((f32[104,128]{1,0:T(8,128)S(1)}, f32[104,128]{1,0:T(8,128)S(1)}, u32[]{:S(2)}, u32[]{:S(2)}) %collective-permute-start) | collective-permute-done | bytes 53280 | tf_op jit(solution)/shard_map/ppermute | solution.py:538
  2.9 2.9 %collective-permute-start.1 = (f32[208,128]{1,0:T(8,128)S(1)}, f32[208,128]{1,0:T(8,128)S(1)}, u32[]{:S(2)}, u32[]{:S(2)}) collective-permute-start(f32[208,128]{1,0:T(8,128)S(1)} %pad_maximum_fusion), channel_id=1, source_target_pairs={{4,2},{5,3},{8,6},{9,7},{12,10},{13,11},{16,14},{17,15},{20,18},{2... | collective-permute-start | bytes 319496 | tf_op jit(solution)/shard_map/ppermute | solution.py:538
  5.8 0.1 collective-permute-start.2
  5.9 1.8 %columns.1 = (f32[32,80,128]{2,1,0:T(8,128)S(1)}, f32[160,128]{1,0:T(8,128)S(1)}) custom-call(f32[32,32]{1,0:T(8,128)} %diffusion.3, f32[32,80,128]{2,1,0:T(8,128)} %bitcast.14, f32[80,128]{1,0:T(8,128)} %bitcast.15, f32[40,40]{1,0:T(8,128)} %salt_matrix.1), custom_call_target="tpu_custom_call" | custom-call | flops 10000000 | bytes 3000000 | tf_op jit(solution)/shard_map/columns/pallas_call | solution.py:575
  7.8 2.0 %collective-permute-done.2.far = f32[64,128]{1,0:T(8,128)S(1)} collective-permute-done((f32[64,128]{1,0:T(8,128)S(1)}, f32[64,128]{1,0:T(8,128)S(1)}, u32[]{:S(2)}, u32[]{:S(2)}) %collective-permute-start.2) | collective-permute-done | bytes 32800 | tf_op jit(solution)/shard_map/ppermute | solution.py:538
  9.8 0.0 collective-permute-done.1.near
  9.8 0.2 collective-permute-start.3
  9.9 1.1 %collective-permute-done.3.inner = f32[208,128]{1,0:T(8,128)S(1)} collective-permute-done((f32[208,128]{1,0:T(8,128)S(1)}, f32[208,128]{1,0:T(8,128)S(1)}, u32[]{:S(2)}, u32[]{:S(2)}) %collective-permute-start.3) | collective-permute-done | bytes 106528 | tf_op jit(solution)/shard_map/ppermute | solution.py:538
  11.1 0.3 %sweeps.1 = (f32[264,128]{1,0:T(8,128)S(1)}, f32[40,128]{1,0:T(8,128)S(1)}) custom-call(f32[160,128]{1,0:T(8,128)S(1)} %get-tuple-element.24.local, f32[104,128]{1,0:T(8,128)S(1)} %pack.1.own, f32[104,128]{1,0:T(8,128)S(1)} %collective-permute-done.partner, f32[208,128]{1,0:T(8,128)S(1)} %collective-permute-done.1.near, ...), custom_call_target="tpu_custom_call" | custom-call | flops 1000000 | bytes 500000 | tf_op jit(solution)/shard_map/sweeps/pallas_call | solution.py:600
  11.3 1.4 %collective-permute-start.4 = (f32[264,128]{1,0:T(8,128)S(1)}, f32[264,128]{1,0:T(8,128)S(1)}, u32[]{:S(2)}, u32[]{:S(2)}) collective-permute-start(f32[264,128]{1,0:T(8,128)S(1)} %get-tuple-element.27.mine), channel_id=1, source_target_pairs={{0,1},{1,0},{2,3},{3,2},{4,5},{5,4},{6,7},{7,6},{8,9},{9,8},{10,11... | collective-permute-start | bytes 405512 | tf_op jit(solution)/shard_map/ppermute | solution.py:538
  12.7 0.0 copy-done.1
  12.7 0.1 copy.16.link
  12.8 0.7 %links.1 = (f32[160,64]{1,0:T(8,128)S(1)}, f32[32,160]{1,0:T(8,128)S(1)}) custom-call(f32[40,16]{1,0:T(8,128)S(1)} %copy.16.link, f32[16,40]{1,0:T(8,128)S(1)} %bitcast.13), custom_call_target="tpu_custom_call" | custom-call | flops 10000000 | bytes 100000 | tf_op jit(solution)/shard_map/links/pallas_call | solution.py:620
  13.5 0.0 copy-done
  13.5 1.6 %grains.1.base = f32[32,80,128]{2,1,0:T(8,128)S(1)} custom-call(f32[32,80,128]{2,1,0:T(8,128)S(1)} %get-tuple-element.31.grain, f32[32,32]{1,0:T(8,128)S(1)} %copy-done), custom_call_target="tpu_custom_call" | custom-call | flops 1000000000 | bytes 3000000 | tf_op jit(solution)/shard_map/grains/pallas_call | solution.py:611
  15.1 2.0 %collective-permute-done.4.other = f32[264,128]{1,0:T(8,128)S(1)} collective-permute-done((f32[264,128]{1,0:T(8,128)S(1)}, f32[264,128]{1,0:T(8,128)S(1)}, u32[]{:S(2)}, u32[]{:S(2)}) %collective-permute-start.4) | collective-permute-done | bytes 135200 | tf_op jit(solution)/shard_map/ppermute | solution.py:538
  17.1 2.5 %reaction.1 = (f32[32,128]{1,0:T(8,128)}, f32[32,128]{1,0:T(8,128)}, f32[32,128]{1,0:T(8,128)}, f32[32,80,128]{2,1,0:T(8,128)}, f32[80,128]{1,0:T(8,128)}) custom-call(f32[32,32]{1,0:T(8,128)} %diffusion.3, f32[264,128]{1,0:T(8,128)S(1)} %get-tuple-element.27.mine, f32[264,128]{1,0:T(8,128)S(1)} %collective-permute-done.4.other, ...), custom_call_target="tpu_custom_call" | custom-call | flops 10000000 | bytes 3000000 | tf_op jit(solution)/shard_map/reaction/pallas_call | solution.py:629
  (2 shorter events, 0.0 us)
Async XLA Ops:
  0.6 12.9 %copy-start = (f32[32,32]{1,0:T(8,128)S(1)}, f32[32,32]{1,0:T(8,128)}, u32[]{:S(2)}) copy-start(f32[32,32]{1,0:T(8,128)} %diffusion.3) | copy-start | bytes 12292
  0.6 12.1 %copy-start.1 = (f32[40,16]{0,1:T(8,128)S(1)}, f32[40,16]{0,1:T(8,128)}, u32[]{:S(2)}) copy-start(f32[40,16]{0,1:T(8,128)} %param.17) | copy-start | bytes 7684
  1.5 1.4 %collective-permute-start = (f32[104,128]{1,0:T(8,128)S(1)}, f32[104,128]{1,0:T(8,128)S(1)}, u32[]{:S(2)}, u32[]{:S(2)}) collective-permute-start(f32[104,128]{1,0:T(8,128)S(1)} %pack.1.own), channel_id=1, source_target_pairs={{0,2},{1,3},{4,6},{5,7},{8,10},{9,11},{12,14},{13,15},{16,18},{17,... | collective-permute-start | bytes 159752 | tf_op jit(solution)/shard_map/ppermute | solution.py:538
  2.9 6.8 %collective-permute-start.1 = (f32[208,128]{1,0:T(8,128)S(1)}, f32[208,128]{1,0:T(8,128)S(1)}, u32[]{:S(2)}, u32[]{:S(2)}) collective-permute-start(f32[208,128]{1,0:T(8,128)S(1)} %pad_maximum_fusion), channel_id=1, source_target_pairs={{4,2},{5,3},{8,6},{9,7},{12,10},{13,11},{16,14},{17,15},{20,18},{2... | collective-permute-start | bytes 319496 | tf_op jit(solution)/shard_map/ppermute | solution.py:538
  5.8 3.9 %collective-permute-start.2 = (f32[64,128]{1,0:T(8,128)S(1)}, f32[64,128]{1,0:T(8,128)S(1)}, u32[]{:S(2)}, u32[]{:S(2)}) collective-permute-start(f32[64,128]{1,0:T(8,128)S(1)} %slice.4), channel_id=1, source_target_pairs={{8,2},{9,3},{12,6},{13,7},{16,10},{17,11},{20,14},{21,15},{24,18},... | collective-permute-start | bytes 98312 | tf_op jit(solution)/shard_map/ppermute | solution.py:538
  9.8 1.3 %collective-permute-start.3 = (f32[208,128]{1,0:T(8,128)S(1)}, f32[208,128]{1,0:T(8,128)S(1)}, u32[]{:S(2)}, u32[]{:S(2)}) collective-permute-start(f32[208,128]{1,0:T(8,128)S(1)} %collective-permute-done.1.near), channel_id=1, source_target_pairs={{0,2},{1,3},{4,6},{5,7},{8,10},{9,11},{12,14},{13,15},{16,18},{17,... | collective-permute-start | bytes 319496 | tf_op jit(solution)/shard_map/ppermute | solution.py:538
  11.3 5.7 %collective-permute-start.4 = (f32[264,128]{1,0:T(8,128)S(1)}, f32[264,128]{1,0:T(8,128)S(1)}, u32[]{:S(2)}, u32[]{:S(2)}) collective-permute-start(f32[264,128]{1,0:T(8,128)S(1)} %get-tuple-element.27.mine), channel_id=1, source_target_pairs={{0,1},{1,0},{2,3},{3,2},{4,5},{5,4},{6,7},{7,6},{8,9},{9,8},{10,11... | collective-permute-start | bytes 405512 | tf_op jit(solution)/shard_map/ppermute | solution.py:538
where the time goes:
time: 19.9 us; the launch traced here: 19.5 us
  Pallas kernels  7.66 us (38%)
  waiting for transfers between devices  6 us (30%)
  starting transfers between devices  5.08 us (26%)
  between operations  0.69 us (3%)
    ppermute x5, waiting for transfers between devices, send(): return lax.ppermute(value, ('tile', 'layer'), pairs)  6 us
    ppermute x5, starting transfers between devices, send(): return lax.ppermute(value, ('tile', 'layer'), pairs)  5.08 us
    pallas_call x1, Pallas kernels, per_device(): call(functools.partial(reaction_kernel, sheets, blocks), 'reaction', (sha...  2.47 us
    pallas_call x1, Pallas kernels, per_device(): call(local_kernel, 'columns', (shaped(shells, nodes, LANES), shaped(2 * n...  1.81 us
    pallas_call x1, Pallas kernels, per_device(): call(grain_kernel, 'grains', shaped(shells, nodes, LANES), [VMEM] * 2, VM...  1.55 us
    pallas_call x1, Pallas kernels, per_device(): call(functools.partial(pack_kernel, blocks), 'pack', shaped(3 * n + edge,...  0.86 us
    pallas_call x1, Pallas kernels, per_device(): call(functools.partial(link_kernel, blocks, 2), 'links', (shaped(points *...  0.72 us
  transfers between devices with their start and end apart: 5, of which 4 were waited for; matrix products, arithmetic and copies ran while one was open for 0% of the time, Pallas kernels for 21%

commit v1 on v0

--- a/solution.py
+++ b/solution.py
@@ -238,17 +238,65 @@
     return high, (value - high.astype(jnp.float32)).astype(jnp.bfloat16)
 
 
+def link_matrices(blocks, parts, turned, links, wide_link, wide_turned):
+    sheets, points = turned.shape
+    per = blocks // parts
+    own = sheets // parts
+    rows, columns = points * blocks, sheets * blocks
+    layer = lax.axis_index("layer")
+    product = functools.partial(
+        lax.dot_general, precision=HIGHEST, preferred_element_type=jnp.float32
+    )
+    plain, across = (((1,), (0,)), ((), ())), (((1,), (1,)), ((), ()))
+
+    def iota(shape):
+        return [lax.broadcasted_iota(jnp.int32, shape, axis) for axis in range(2)]
+
+    def fits(r, c):
+        part = lax.rem(r // (points * per) + layer, parts)
+        return lax.rem(c, blocks) == part * per + lax.rem(r, per)
+
+    r, c = iota((rows, points))
+    pick = (lax.rem(r, points * per) // per == c).astype(jnp.float32)
+    r, c = iota((sheets, columns))
+    split = (c // blocks == r).astype(jnp.float32)
+    full = product(product(pick, links[...], across), split, plain)
+    r, c = iota((rows, columns))
+    wide_link[...] = jnp.where(fits(r, c), full, 0.0)
+    r, c = iota((own * blocks, sheets))
+    split = (r // blocks + own * layer == c).astype(jnp.float32)
+    full = product(product(split, links[...], plain), pick, across)
+    r, c = iota((own * blocks, rows))
+    wide_turned[...] = jnp.where(fits(c, r), full, 0.0)
+
+
 def local_kernel(
-    diffusion, grain, salt, salt_matrix, held, local, weights, level, matrix, sems, grain_sems
+    blocks,
+    parts,
+    diffusion,
+    grain,
+    salt,
+    salt_matrix,
+    turned,
+    held,
+    local,
+    wide_link,
+    wide_turned,
+    factors,
+    weights,
+    level,
+    matrix,
+    links,
+    sems,
+    grain_sems,
 ):
     shells, nodes, _ = grain.shape
     part = shells // grain_sems.shape[0]
-    small = fetch(((salt, level), (salt_matrix, matrix), (diffusion, weights)), sems)
+    small = fetch(
+        ((salt, level), (salt_matrix, matrix), (diffusion, weights), (turned, links)), sems
+    )
     copies = fetch(
-        [
-            (grain.at[s : s + part], held.at[s : s + part])
-            for s in range(0, shells, part)
-        ],
+        [(grain.at[s : s + part], held.at[s : s + part]) for s in range(0, shells, part)],
         grain_sems,
     )
     for copy in small:
@@ -259,6 +307,11 @@
         precision=HIGHEST,
         preferred_element_type=jnp.float32,
     )
+    link_matrices(blocks, parts, turned, links, wide_link, wide_turned)
+    for shell in range(shells):
+        factors[shell : shell + 1, :] = jnp.full(
+            (1, LANES), shell_flux * weights[shell, shells - 1]
+        )
     surface = jnp.zeros((nodes, LANES), jnp.float32)
     for i, copy in enumerate(copies):
         copy.wait()
@@ -267,10 +320,10 @@
     local[0:nodes, :] = surface
 
 
-def grain_kernel(grain, shells_matrix, base):
-    shells, nodes, _ = grain.shape
-    matrix_high, matrix_low = halves(wide(shells_matrix[...], ROWS))
-    for start in range(0, nodes, 2 * ROWS):
+def grain_kernel(grain, weights, base):
+    shells, count, _ = grain.shape
+    matrix_high, matrix_low = halves(wide(weights[...], ROWS))
+    for start in range(0, count, 2 * ROWS):
         pair = [
             grain[:, start + k * ROWS : start + (k + 1) * ROWS, :].reshape(shells * ROWS, LANES)
             for k in range(2)
@@ -283,7 +336,7 @@
             base[:, start + k * ROWS : start + (k + 1) * ROWS, :] = part
 
 
-def sweep_kernel(sheets, blocks, tiles, local, own, partner, near, far, inner, out, masks):
+def sweep_kernel(sheets, blocks, tiles, own, partner, near, far, inner, out, masks):
     n = sheets * blocks
     size = own.shape[0]
     tile = lax.axis_index("tile")
@@ -338,7 +391,6 @@
             edge = jnp.where(block == 0, value[n - blocks :, :], value[0:blocks, :])
             start = 2 * n + (2 * i + k) * blocks
             out[start : start + blocks, :] = edge
-    out[2 * n + 10 * blocks :, :] = local[...]
 
 
 def react(surface_base, gain, rate, node_voltage):
@@ -354,9 +406,11 @@
 def reaction_kernel(
     sheets,
     blocks,
-    diffusion,
+    factors,
     mine,
     other,
+    local,
+    other_local,
     masks,
     base,
     link,
@@ -366,7 +420,6 @@
     flux,
     grain_out,
     salt_out,
-    weights,
     both,
     sheets_now,
     copy_out,
@@ -377,8 +430,7 @@
     shells, nodes, _ = base.shape
     block = lax.axis_index("layer")
     edge = 2 * blocks
-    start = 2 * n + 5 * edge
-    early = fetch(((diffusion, weights), (mine.at[start + nodes : start + 2 * nodes], salt_out)), sems)
+    early = fetch(((local.at[nodes : 2 * nodes], salt_out),), sems)
 
     free = [masks[i * edge : (i + 1) * edge, :] for i in range(5)]
     added = []
@@ -406,76 +458,39 @@
     extra = jnp.concatenate([added[2], volt[0]], axis=1)
     extra = jnp.where(block == 0, extra, pltpu.roll(extra, blocks, 0))
     both[n - blocks : n + blocks, :] += extra
-    warmth_copy = pltpu.make_async_copy(both.at[here, 0:LANES], next_warmth, sems.at[2])
+    warmth_copy = pltpu.make_async_copy(both.at[here, 0:LANES], next_warmth, sems.at[1])
     warmth_copy.start()
 
     dot = functools.partial(jnp.dot, precision=HIGHEST, preferred_element_type=jnp.float32)
     node = dot(link[...], both[...])
-    early[0].wait()
-    gain = shell_flux * weights[shells - 1, shells - 1]
-    results = []
-    for part, ref in enumerate((mine, other)):
-        rows = slice(part * nodes, (part + 1) * nodes)
-        node_temp, node_voltage = node[rows, 0:LANES], node[rows, LANES:]
-        surface_base = ref[start : start + nodes, :]
-        salt = ref[start + nodes : start + 2 * nodes, :]
-        rate = 1.0 / ((1.0 + jnp.exp(-0.3 * node_temp)) * (1.0 + jnp.exp(-salt)))
-        results.append(react(surface_base, gain, rate, node_voltage))
-        if part == 0:
-            reaction = results[0][0]
-            copies = []
-            step = shells // grain_sems.shape[0]
-            for first in range(0, shells, step):
-                for shell in range(first, first + step):
-                    factor = shell_flux * weights[shell, shells - 1]
-                    copy_out[shell] = base[shell] - factor * reaction
-                copies.append(
-                    pltpu.make_async_copy(
-                        copy_out.at[first : first + step],
-                        grain_out.at[first : first + step],
-                        grain_sems.at[first // step],
-                    )
-                )
-                copies[-1].start()
-    columns = jnp.concatenate([jnp.concatenate(r[::-1], axis=1) for r in results], axis=0)
-    sheets_now[...] = dot(turned[...], columns)
+    gain = factors[shells - 1 :, :]
+    surface_base = jnp.concatenate([local[0:nodes, :], other_local[0:nodes, :]], axis=0)
+    salt = jnp.concatenate([local[nodes:, :], other_local[nodes:, :]], axis=0)
+    rate = 1.0 / ((1.0 + jnp.exp(-0.3 * node[:, 0:LANES])) * (1.0 + jnp.exp(-salt)))
+    reaction, source = react(surface_base, gain, rate, node[:, LANES:])
+    sheets_now[...] = dot(turned[...], jnp.concatenate([source, reaction], axis=1))
     late = [
-        pltpu.make_async_copy(sheets_now.at[:, 0:LANES], warming, sems.at[3]),
-        pltpu.make_async_copy(sheets_now.at[:, LANES:], flux, sems.at[4]),
+        pltpu.make_async_copy(sheets_now.at[:, 0:LANES], warming, sems.at[2]),
+        pltpu.make_async_copy(sheets_now.at[:, LANES:], flux, sems.at[3]),
     ]
     for copy in late:
         copy.start()
-    for copy in early[1:] + [warmth_copy] + copies + late:
+    copies = []
+    step = shells // grain_sems.shape[0]
+    for first in range(0, shells, step):
+        for shell in range(first, first + step):
+            factor = factors[shell : shell + 1, :]
+            copy_out[shell] = base[shell] - factor * reaction[0:nodes, :]
+        copies.append(
+            pltpu.make_async_copy(
+                copy_out.at[first : first + step],
+                grain_out.at[first : first + step],
+                grain_sems.at[first // step],
+            )
+        )
+        copies[-1].start()
+    for copy in early + [warmth_copy] + copies + late:
         copy.wait()
-
-
-def link_kernel(blocks, parts, link, turned, wide_link, wide_turned):
-    nodes, sheets = link.shape
-    per = blocks // parts
-    own = sheets // parts
-    rows, columns = nodes * blocks, sheets * blocks
-    layer = lax.axis_index("layer")
-    dot = functools.partial(jnp.dot, precision=HIGHEST, preferred_element_type=jnp.float32)
-
-    def iota(shape):
-        return [lax.broadcasted_iota(jnp.int32, shape, axis) for axis in range(2)]
-
-    def fits(r, c):
-        part = lax.rem(r // (nodes * per) + layer, parts)
-        return lax.rem(c, blocks) == part * per + lax.rem(r, per)
-
-    r, c = iota((rows, nodes))
-    pick = (lax.rem(r, nodes * per) // per == c).astype(jnp.float32)
-    r, c = iota((sheets, columns))
-    split = (c // blocks == r).astype(jnp.float32)
-    r, c = iota((rows, columns))
-    wide_link[...] = jnp.where(fits(r, c), dot(dot(pick, link[...]), split), 0.0)
-    r, c = iota((nodes, rows))
-    pick = (lax.rem(c, nodes * per) // per == r).astype(jnp.float32)
-    r, c = iota((own * blocks, sheets))
-    split = (r // blocks + own * layer == c).astype(jnp.float32)
-    r, c = iota((own * blocks, rows))
-    wide_turned[...] = jnp.where(fits(c, r), dot(dot(split, turned[...]), pick), 0.0)
 
 
 VMEM = pl.BlockSpec(memory_space=pltpu.VMEM)
@@ -572,19 +587,26 @@
     partner = send(own, cores)
     near = send(jnp.concatenate([own, partner], axis=0), beside)
     far = send(own[0 : 2 * n], beyond)
-    held, local = call(
-        local_kernel,
+    held, local, link, turned, factors = call(
+        functools.partial(local_kernel, blocks, 2),
         "columns",
-        (shaped(shells, nodes, LANES), shaped(2 * nodes, LANES)),
-        [HBM] * 4,
-        (VMEM, VMEM),
+        (
+            shaped(shells, nodes, LANES),
+            shaped(2 * nodes, LANES),
+            shaped(points * blocks, 2 * n),
+            shaped(n, points * blocks),
+            shaped(shells, LANES),
+        ),
+        [HBM] * 5,
+        (VMEM,) * 5,
         10**7,
         3000000,
         (
             pltpu.SMEM(grain_diffusion_matrix.shape, jnp.float32),
             pltpu.VMEM((nodes, LANES), jnp.float32),
             pltpu.VMEM(solution_diffusion_matrix.shape, jnp.float32),
-            pltpu.SemaphoreType.DMA((3,)),
+            pltpu.VMEM(sheet_node_link_matrix.shape[::-1], jnp.float32),
+            pltpu.SemaphoreType.DMA((4,)),
             pltpu.SemaphoreType.DMA((4,)),
         ),
     )(
@@ -593,39 +615,26 @@
             grain_shell_level.reshape(shells, nodes, LANES),
             solution_salt_level.reshape(nodes, LANES),
             solution_diffusion_matrix,
+            sheet_node_link_matrix.T,
         )
     )
+    other_local = send(local, layers)
     near, far, held, local = lax.optimization_barrier((near, far, held, local))
     inner = send(near, cores)
     mine, masks = call(
         functools.partial(sweep_kernel, sheets, blocks, tiles),
         "sweeps",
-        (shaped(2 * n + 5 * edge + 2 * nodes, LANES), shaped(5 * edge, LANES)),
-        [VMEM] * 6,
+        (shaped(2 * n + 5 * edge, LANES), shaped(5 * edge, LANES)),
+        [VMEM] * 5,
         (VMEM, VMEM),
         10**6,
         500000,
-    )(local, own, partner, near, far, inner)
+    )(own, partner, near, far, inner)
     other = send(mine, layers)
     held, masks = lax.optimization_barrier((held, masks))
     base = call(
-        grain_kernel,
-        "grains",
-        shaped(shells, nodes, LANES),
-        [VMEM] * 2,
-        VMEM,
-        10**9,
-        3000000,
+        grain_kernel, "grains", shaped(shells, nodes, LANES), [VMEM] * 2, VMEM, 10**9, 3000000
     )(held, grain_diffusion_matrix)
-    link, turned = call(
-        functools.partial(link_kernel, blocks, 2),
-        "links",
-        (shaped(points * blocks, 2 * n), shaped(n, points * blocks)),
-        [VMEM] * 2,
-        (VMEM, VMEM),
-        10**7,
-        100000,
-    )(sheet_node_link_matrix, sheet_node_link_matrix.T)
     next_warmth, warming, flux, grain, salt = call(
         functools.partial(reaction_kernel, sheets, blocks),
         "reaction",
@@ -636,19 +645,18 @@
             shaped(shells, nodes, LANES),
             shaped(nodes, LANES),
         ),
-        [HBM] + [VMEM] * 6,
+        [VMEM] * 9,
         (HBM,) * 5,
         10**7,
         3000000,
         (
-            pltpu.SMEM(grain_diffusion_matrix.shape, jnp.float32),
             pltpu.VMEM((2 * n, 2 * LANES), jnp.float32),
             pltpu.VMEM((n, 2 * LANES), jnp.float32),
             pltpu.VMEM((shells, nodes, LANES), jnp.float32),
-            pltpu.SemaphoreType.DMA((5,)),
+            pltpu.SemaphoreType.DMA((4,)),
             pltpu.SemaphoreType.DMA((4,)),
         ),
-    )(*in_hbm(grain_diffusion_matrix), mine, other, masks, base, link, turned)
+    )(factors, mine, other, local, other_local, masks, base, link, turned)
     return (
         next_warmth.reshape(warmth_level.shape),
         warming.reshape(warmth_level.shape),

time: 19.9 us -> 18 us (0.905)
  waiting for transfers between devices: 6 us -> 3.92 us
  starting transfers between devices: 5.08 us -> 6.21 us
  Pallas kernels: 7.66 us -> 6.95 us
    ppermute x5 -> x6, waiting for transfers between devices: 6 us -> 3.92 us  [send(): return lax.ppermute(value, ('tile', 'layer'), pairs)]
    ppermute x5 -> x6, starting transfers between devices: 5.08 us -> 6.21 us  [send(): return lax.ppermute(value, ('tile', 'layer'), pairs)]
    pallas_call x1, Pallas kernels: 2.47 us -> 1.89 us  [per_device(): call(functools.partial(reaction_kernel, sheets, blocks), 'reaction', (sha...]
    pallas_call x2 -> x1, Pallas kernels: 2.53 us -> 2.39 us  [per_device(): call(functools.partial(local_kernel, blocks, 2), 'columns', (shaped(shell...]
  transfers between devices with their start and end apart: 5 -> 6, of which waited for: 4 -> 4; matrix products, arithmetic and copies ran while one was open for 0% -> 0% of each run, Pallas kernels for 21% -> 24%
where the time goes in v1:
time: 18 us; the launch traced here: 17.8 us
  Pallas kernels  6.95 us (39%)
  starting transfers between devices  6.21 us (34%)
  waiting for transfers between devices  3.92 us (22%)
  between operations  0.68 us (4%)
    ppermute x6, starting transfers between devices, send(): return lax.ppermute(value, ('tile', 'layer'), pairs)  6.21 us
    ppermute x6, waiting for transfers between devices, send(): return lax.ppermute(value, ('tile', 'layer'), pairs)  3.92 us
    pallas_call x1, Pallas kernels, per_device(): call(functools.partial(local_kernel, blocks, 2), 'columns', (shaped(shell...  2.39 us
    pallas_call x1, Pallas kernels, per_device(): call(functools.partial(reaction_kernel, sheets, blocks), 'reaction', (sha...  1.89 us
    pallas_call x1, Pallas kernels, per_device(): call(grain_kernel, 'grains', shaped(shells, nodes, LANES), [VMEM] * 2, VM...  1.56 us
    pallas_call x1, Pallas kernels, per_device(): call(functools.partial(pack_kernel, blocks), 'pack', shaped(3 * n + edge,...  0.86 us
  transfers between devices with their start and end apart: 6, of which 4 were waited for; matrix products, arithmetic and copies ran while one was open for 0% of the time, Pallas kernels for 24%

profile of v1, /device:TPU:0, one launch (start us, length us, event | category | flops | bytes accessed | tf_op | source)
XLA Modules:
  0.0 17.8 jit_solution(10157076331907840100)
XLA Ops:
  0.6 0.0 copy-start
  0.6 0.9 %pack.1.own = f32[104,128]{1,0:T(8,128)S(1)} custom-call(f32[4]{0:T(128)} %storage.1, f32[32,128]{1,0:T(8,128)} %bitcast.15, f32[32,128]{1,0:T(8,128)} %bitcast.16, s32[32,128]{1,0:T(8,128)} %bitcast.17, f32[32,128]{1,0:T(8,128)} %bitcast.18, s32[4,128]{1,0:T(4,128)} %bitcast.20), custom_call_target="tpu_custom_call" | custom-call | flops 1000 | bytes 100000 | tf_op jit(solution)/shard_map/pack/pallas_call | solution.py:562
  1.5 0.5 %collective-permute-start = (f32[104,128]{1,0:T(8,128)S(1)}, f32[104,128]{1,0:T(8,128)S(1)}, u32[]{:S(2)}, u32[]{:S(2)}) collective-permute-start(f32[104,128]{1,0:T(8,128)S(1)} %pack.1.own), channel_id=1, source_target_pairs={{0,2},{1,3},{4,6},{5,7},{8,10},{9,11},{12,14},{13,15},{16,18},{17,... | collective-permute-start | bytes 159752 | tf_op jit(solution)/shard_map/ppermute | solution.py:553
  2.0 0.9 %collective-permute-done.partner = f32[104,128]{1,0:T(8,128)S(1)} collective-permute-done((f32[104,128]{1,0:T(8,128)S(1)}, f32[104,128]{1,0:T(8,128)S(1)}, u32[]{:S(2)}, u32[]{:S(2)}) %collective-permute-start) | collective-permute-done | bytes 53280 | tf_op jit(solution)/shard_map/ppermute | solution.py:553
  2.9 2.9 %collective-permute-start.1 = (f32[208,128]{1,0:T(8,128)S(1)}, f32[208,128]{1,0:T(8,128)S(1)}, u32[]{:S(2)}, u32[]{:S(2)}) collective-permute-start(f32[208,128]{1,0:T(8,128)S(1)} %pad_maximum_fusion), channel_id=1, source_target_pairs={{4,2},{5,3},{8,6},{9,7},{12,10},{13,11},{16,14},{17,15},{20,18},{2... | collective-permute-start | bytes 319496 | tf_op jit(solution)/shard_map/ppermute | solution.py:553
  5.8 0.1 collective-permute-start.2
  5.9 2.4 %columns.1 = (f32[32,80,128]{2,1,0:T(8,128)S(1)}, f32[160,128]{1,0:T(8,128)S(1)}, f32[160,64]{1,0:T(8,128)S(1)}, f32[32,160]{1,0:T(8,128)S(1)}, f32[32,128]{1,0:T(8,128)S(1)}) custom-call(f32[32,32]{1,0:T(8,128)} %weights.1, f32[32,80,128]{2,1,0:T(8,128)} %bitcast.13, f32[80,128]{1,0:T(8,128)} %bitcast.14, f32[40,40]{1,0:T(8,128)} %salt_matrix.1, ...), custom_call_target="tpu_custom_call" | custom-call | flops 10000000 | bytes 3000000 | tf_op jit(solution)/shard_map/columns/pallas_call | solution.py:590
  8.3 1.4 %collective-permute-done.2.far = f32[64,128]{1,0:T(8,128)S(1)} collective-permute-done((f32[64,128]{1,0:T(8,128)S(1)}, f32[64,128]{1,0:T(8,128)S(1)}, u32[]{:S(2)}, u32[]{:S(2)}) %collective-permute-start.2) | collective-permute-done | bytes 32800 | tf_op jit(solution)/shard_map/ppermute | solution.py:553
  9.8 0.0 collective-permute-done.1.near
  9.8 0.2 %collective-permute-start.3 = (f32[208,128]{1,0:T(8,128)S(1)}, f32[208,128]{1,0:T(8,128)S(1)}, u32[]{:S(2)}, u32[]{:S(2)}) collective-permute-start(f32[208,128]{1,0:T(8,128)S(1)} %collective-permute-done.1.near), channel_id=1, source_target_pairs={{0,2},{1,3},{4,6},{5,7},{8,10},{9,11},{12,14},{13,15},{16,18},{17,... | collective-permute-start | bytes 319496 | tf_op jit(solution)/shard_map/ppermute | solution.py:553
  9.9 1.5 %collective-permute-start.5 = (f32[160,128]{1,0:T(8,128)S(1)}, f32[160,128]{1,0:T(8,128)S(1)}, u32[]{:S(2)}, u32[]{:S(2)}) collective-permute-start(f32[160,128]{1,0:T(8,128)S(1)} %get-tuple-element.29.local), channel_id=1, source_target_pairs={{0,1},{1,0},{2,3},{3,2},{4,5},{5,4},{6,7},{7,6},{8,9},{9,8},{10,11... | collective-permute-start | bytes 245768 | tf_op jit(solution)/shard_map/ppermute | solution.py:553
  11.4 0.0 collective-permute-done.3.inner
  11.4 0.3 %sweeps.1 = (f32[104,128]{1,0:T(8,128)S(1)}, f32[40,128]{1,0:T(8,128)S(1)}) custom-call(f32[104,128]{1,0:T(8,128)S(1)} %pack.1.own, f32[104,128]{1,0:T(8,128)S(1)} %collective-permute-done.partner, f32[208,128]{1,0:T(8,128)S(1)} %collective-permute-done.1.near, f32[64,128]{1,0:T(8,128)S(1)} %collective-permute-done.2.far, ...), custom_call_target="tpu_custom_call" | custom-call | flops 1000000 | bytes 500000 | tf_op jit(solution)/shard_map/sweeps/pallas_call | solution.py:624
  11.7 1.0 %collective-permute-start.4 = (f32[104,128]{1,0:T(8,128)S(1)}, f32[104,128]{1,0:T(8,128)S(1)}, u32[]{:S(2)}, u32[]{:S(2)}) collective-permute-start(f32[104,128]{1,0:T(8,128)S(1)} %get-tuple-element.28.mine), channel_id=1, source_target_pairs={{0,1},{1,0},{2,3},{3,2},{4,5},{5,4},{6,7},{7,6},{8,9},{9,8},{10,11... | collective-permute-start | bytes 159752 | tf_op jit(solution)/shard_map/ppermute | solution.py:553
  12.7 0.0 copy-done
  12.7 1.6 %grains.1.base = f32[32,80,128]{2,1,0:T(8,128)S(1)} custom-call(f32[32,80,128]{2,1,0:T(8,128)S(1)} %get-tuple-element.33.grain, f32[32,32]{1,0:T(8,128)S(1)} %copy-done), custom_call_target="tpu_custom_call" | custom-call | flops 1000000000 | bytes 3000000 | tf_op jit(solution)/shard_map/grains/pallas_call | solution.py:635
  14.3 0.8 %collective-permute-done.5.other_local = f32[160,128]{1,0:T(8,128)S(1)} collective-permute-done((f32[160,128]{1,0:T(8,128)S(1)}, f32[160,128]{1,0:T(8,128)S(1)}, u32[]{:S(2)}, u32[]{:S(2)}) %collective-permute-start.5) | collective-permute-done | bytes 81952 | tf_op jit(solution)/shard_map/ppermute | solution.py:553
  15.1 0.8 %collective-permute-done.4.other = f32[104,128]{1,0:T(8,128)S(1)} collective-permute-done((f32[104,128]{1,0:T(8,128)S(1)}, f32[104,128]{1,0:T(8,128)S(1)}, u32[]{:S(2)}, u32[]{:S(2)}) %collective-permute-start.4) | collective-permute-done | bytes 53280 | tf_op jit(solution)/shard_map/ppermute | solution.py:553
  15.9 1.9 %reaction.1 = (f32[32,128]{1,0:T(8,128)}, f32[32,128]{1,0:T(8,128)}, f32[32,128]{1,0:T(8,128)}, f32[32,80,128]{2,1,0:T(8,128)}, f32[80,128]{1,0:T(8,128)}) custom-call(f32[32,128]{1,0:T(8,128)S(1)} %get-tuple-element.23.factors, f32[104,128]{1,0:T(8,128)S(1)} %get-tuple-element.28.mine, f32[104,128]{1,0:T(8,128)S(1)} %collective-permute-done.4.other, ...), custom_call_target="tpu_custom_call" | custom-call | flops 10000000 | bytes 3000000 | tf_op jit(solution)/shard_map/reaction/pallas_call | solution.py:638
  (2 shorter events, 0.0 us)
Async XLA Ops:
  0.6 12.1 %copy-start = (f32[32,32]{1,0:T(8,128)S(1)}, f32[32,32]{1,0:T(8,128)}, u32[]{:S(2)}) copy-start(f32[32,32]{1,0:T(8,128)} %weights.1) | copy-start | bytes 12292
  1.5 1.4 %collective-permute-start = (f32[104,128]{1,0:T(8,128)S(1)}, f32[104,128]{1,0:T(8,128)S(1)}, u32[]{:S(2)}, u32[]{:S(2)}) collective-permute-start(f32[104,128]{1,0:T(8,128)S(1)} %pack.1.own), channel_id=1, source_target_pairs={{0,2},{1,3},{4,6},{5,7},{8,10},{9,11},{12,14},{13,15},{16,18},{17,... | collective-permute-start | bytes 159752 | tf_op jit(solution)/shard_map/ppermute | solution.py:553
  2.9 6.8 %collective-permute-start.1 = (f32[208,128]{1,0:T(8,128)S(1)}, f32[208,128]{1,0:T(8,128)S(1)}, u32[]{:S(2)}, u32[]{:S(2)}) collective-permute-start(f32[208,128]{1,0:T(8,128)S(1)} %pad_maximum_fusion), channel_id=1, source_target_pairs={{4,2},{5,3},{8,6},{9,7},{12,10},{13,11},{16,14},{17,15},{20,18},{2... | collective-permute-start | bytes 319496 | tf_op jit(solution)/shard_map/ppermute | solution.py:553
  5.8 3.9 %collective-permute-start.2 = (f32[64,128]{1,0:T(8,128)S(1)}, f32[64,128]{1,0:T(8,128)S(1)}, u32[]{:S(2)}, u32[]{:S(2)}) collective-permute-start(f32[64,128]{1,0:T(8,128)S(1)} %slice.4), channel_id=1, source_target_pairs={{8,2},{9,3},{12,6},{13,7},{16,10},{17,11},{20,14},{21,15},{24,18},... | collective-permute-start | bytes 98312 | tf_op jit(solution)/shard_map/ppermute | solution.py:553
  9.8 1.7 %collective-permute-start.3 = (f32[208,128]{1,0:T(8,128)S(1)}, f32[208,128]{1,0:T(8,128)S(1)}, u32[]{:S(2)}, u32[]{:S(2)}) collective-permute-start(f32[208,128]{1,0:T(8,128)S(1)} %collective-permute-done.1.near), channel_id=1, source_target_pairs={{0,2},{1,3},{4,6},{5,7},{8,10},{9,11},{12,14},{13,15},{16,18},{17,... | collective-permute-start | bytes 319496 | tf_op jit(solution)/shard_map/ppermute | solution.py:553
  9.9 5.2 %collective-permute-start.5 = (f32[160,128]{1,0:T(8,128)S(1)}, f32[160,128]{1,0:T(8,128)S(1)}, u32[]{:S(2)}, u32[]{:S(2)}) collective-permute-start(f32[160,128]{1,0:T(8,128)S(1)} %get-tuple-element.29.local), channel_id=1, source_target_pairs={{0,1},{1,0},{2,3},{3,2},{4,5},{5,4},{6,7},{7,6},{8,9},{9,8},{10,11... | collective-permute-start | bytes 245768 | tf_op jit(solution)/shard_map/ppermute | solution.py:553
  11.7 4.2 %collective-permute-start.4 = (f32[104,128]{1,0:T(8,128)S(1)}, f32[104,128]{1,0:T(8,128)S(1)}, u32[]{:S(2)}, u32[]{:S(2)}) collective-permute-start(f32[104,128]{1,0:T(8,128)S(1)} %get-tuple-element.28.mine), channel_id=1, source_target_pairs={{0,1},{1,0},{2,3},{3,2},{4,5},{5,4},{6,7},{7,6},{8,9},{9,8},{10,11... | collective-permute-start | bytes 159752 | tf_op jit(solution)/shard_map/ppermute | solution.py:553

commit v2 on v1

--- a/solution.py
+++ b/solution.py
@@ -238,7 +238,7 @@
     return high, (value - high.astype(jnp.float32)).astype(jnp.bfloat16)
 
 
-def link_matrices(blocks, parts, turned, links, wide_link, wide_turned):
+def link_kernel(blocks, parts, turned, wide_link, wide_turned):
     sheets, points = turned.shape
     per = blocks // parts
     own = sheets // parts
@@ -260,54 +260,50 @@
     pick = (lax.rem(r, points * per) // per == c).astype(jnp.float32)
     r, c = iota((sheets, columns))
     split = (c // blocks == r).astype(jnp.float32)
-    full = product(product(pick, links[...], across), split, plain)
+    full = product(product(pick, turned[...], across), split, plain)
     r, c = iota((rows, columns))
     wide_link[...] = jnp.where(fits(r, c), full, 0.0)
     r, c = iota((own * blocks, sheets))
     split = (r // blocks + own * layer == c).astype(jnp.float32)
-    full = product(product(split, links[...], plain), pick, across)
+    full = product(product(split, turned[...], plain), pick, across)
     r, c = iota((own * blocks, rows))
     wide_turned[...] = jnp.where(fits(c, r), full, 0.0)
 
 
 def local_kernel(
-    blocks,
-    parts,
     diffusion,
     grain,
     salt,
     salt_matrix,
-    turned,
     held,
     local,
-    wide_link,
-    wide_turned,
     factors,
     weights,
     level,
     matrix,
-    links,
     sems,
     grain_sems,
 ):
     shells, nodes, _ = grain.shape
     part = shells // grain_sems.shape[0]
-    small = fetch(
-        ((salt, level), (salt_matrix, matrix), (diffusion, weights), (turned, links)), sems
-    )
+    small = fetch(((salt, level), (salt_matrix, matrix), (diffusion, weights)), sems)
     copies = fetch(
         [(grain.at[s : s + part], held.at[s : s + part]) for s in range(0, shells, part)],
         grain_sems,
     )
     for copy in small:
         copy.wait()
-    local[nodes : 2 * nodes, :] = jnp.dot(
-        wide(matrix[...], nodes // matrix.shape[0]),
-        level[...],
+    points = matrix.shape[0]
+    per = nodes // points
+    spans = [level[pl.ds(i, points, stride=per), :] for i in range(per)]
+    spans = jnp.dot(
+        matrix[...],
+        jnp.concatenate(spans, axis=1),
         precision=HIGHEST,
         preferred_element_type=jnp.float32,
     )
-    link_matrices(blocks, parts, turned, links, wide_link, wide_turned)
+    for i in range(per):
+        local[pl.ds(nodes + i, points, stride=per), :] = spans[:, i * LANES : (i + 1) * LANES]
     for shell in range(shells):
         factors[shell : shell + 1, :] = jnp.full(
             (1, LANES), shell_flux * weights[shell, shells - 1]
@@ -465,7 +461,9 @@
     node = dot(link[...], both[...])
     gain = factors[shells - 1 :, :]
     surface_base = jnp.concatenate([local[0:nodes, :], other_local[0:nodes, :]], axis=0)
-    salt = jnp.concatenate([local[nodes:, :], other_local[nodes:, :]], axis=0)
+    salt = jnp.concatenate(
+        [local[nodes : 2 * nodes, :], other_local[nodes : 2 * nodes, :]], axis=0
+    )
     rate = 1.0 / ((1.0 + jnp.exp(-0.3 * node[:, 0:LANES])) * (1.0 + jnp.exp(-salt)))
     reaction, source = react(surface_base, gain, rate, node[:, LANES:])
     sheets_now[...] = dot(turned[...], jnp.concatenate([source, reaction], axis=1))
@@ -539,6 +537,7 @@
     nodes = points * part // LANES
     n = sheets * blocks
     edge = 2 * blocks
+    size = 3 * n + edge
 
     def both_layers(pairs):
         return [(s * 2 + j, t * 2 + j) for s, t in pairs for j in range(2)]
@@ -587,26 +586,23 @@
     partner = send(own, cores)
     near = send(jnp.concatenate([own, partner], axis=0), beside)
     far = send(own[0 : 2 * n], beyond)
-    held, local, link, turned, factors = call(
-        functools.partial(local_kernel, blocks, 2),
+    held, local, factors = call(
+        local_kernel,
         "columns",
         (
             shaped(shells, nodes, LANES),
-            shaped(2 * nodes, LANES),
-            shaped(points * blocks, 2 * n),
-            shaped(n, points * blocks),
+            shaped(2 * nodes + 2 * ROWS, LANES),
             shaped(shells, LANES),
         ),
-        [HBM] * 5,
-        (VMEM,) * 5,
+        [HBM] * 4,
+        (VMEM,) * 3,
         10**7,
         3000000,
         (
             pltpu.SMEM(grain_diffusion_matrix.shape, jnp.float32),
             pltpu.VMEM((nodes, LANES), jnp.float32),
             pltpu.VMEM(solution_diffusion_matrix.shape, jnp.float32),
-            pltpu.VMEM(sheet_node_link_matrix.shape[::-1], jnp.float32),
-            pltpu.SemaphoreType.DMA((4,)),
+            pltpu.SemaphoreType.DMA((3,)),
             pltpu.SemaphoreType.DMA((4,)),
         ),
     )(
@@ -615,12 +611,22 @@
             grain_shell_level.reshape(shells, nodes, LANES),
             solution_salt_level.reshape(nodes, LANES),
             solution_diffusion_matrix,
-            sheet_node_link_matrix.T,
         )
     )
     other_local = send(local, layers)
-    near, far, held, local = lax.optimization_barrier((near, far, held, local))
-    inner = send(near, cores)
+    near, far, held, local, turned = lax.optimization_barrier(
+        (near, far, held, local, sheet_node_link_matrix.T)
+    )
+    link, turned = call(
+        functools.partial(link_kernel, blocks, 2),
+        "links",
+        (shaped(points * blocks, 2 * n), shaped(n, points * blocks)),
+        [VMEM],
+        (VMEM, VMEM),
+        10**6,
+        100000,
+    )(turned)
+    inner = send(near[0 : size + 2 * n], cores)
     mine, masks = call(
         functools.partial(sweep_kernel, sheets, blocks, tiles),
         "sweeps",
@@ -631,7 +637,7 @@
         500000,
     )(own, partner, near, far, inner)
     other = send(mine, layers)
-    held, masks = lax.optimization_barrier((held, masks))
+    held, masks, other_local = lax.optimization_barrier((held, masks, other_local))
     base = call(
         grain_kernel, "grains", shaped(shells, nodes, LANES), [VMEM] * 2, VMEM, 10**9, 3000000
     )(held, grain_diffusion_matrix)

time: 18 us -> 17.7 us (0.983)
  waiting for transfers between devices: 3.92 us -> 2.84 us
  starting transfers between devices: 6.21 us -> 7.14 us
  Pallas kernels: 6.95 us -> 6.76 us
    ppermute x6, waiting for transfers between devices: 3.92 us -> 2.84 us  [send(): return lax.ppermute(value, ('tile', 'layer'), pairs)]
    ppermute x6, starting transfers between devices: 6.21 us -> 7.14 us  [send(): return lax.ppermute(value, ('tile', 'layer'), pairs)]
    pallas_call x1 -> x2, Pallas kernels: 2.39 us -> 2.19 us  [the longest x1 1.4 us: per_device(): call(local_kernel, 'columns', (shaped(shells, nodes, LANES), shaped(2 * n...]
  transfers between devices with their start and end apart: 6 -> 6, of which waited for: 4 -> 4; matrix products, arithmetic and copies ran while one was open for 0% -> 0% of each run, Pallas kernels for 24% -> 23%
where the time goes in v2:
time: 17.7 us; the launch traced here: 17.5 us
  starting transfers between devices  7.14 us (40%)
  Pallas kernels  6.76 us (38%)
  waiting for transfers between devices  2.84 us (16%)
  between operations  0.71 us (4%)
    ppermute x6, starting transfers between devices, send(): return lax.ppermute(value, ('tile', 'layer'), pairs)  7.14 us
    ppermute x6, waiting for transfers between devices, send(): return lax.ppermute(value, ('tile', 'layer'), pairs)  2.84 us
    pallas_call x1, Pallas kernels, per_device(): call(functools.partial(reaction_kernel, sheets, blocks), 'reaction', (sha...  1.88 us
    pallas_call x1, Pallas kernels, per_device(): call(grain_kernel, 'grains', shaped(shells, nodes, LANES), [VMEM] * 2, VM...  1.57 us
    pallas_call x1, Pallas kernels, per_device(): call(local_kernel, 'columns', (shaped(shells, nodes, LANES), shaped(2 * n...  1.4 us
    pallas_call x1, Pallas kernels, per_device(): call(functools.partial(pack_kernel, blocks), 'pack', shaped(3 * n + edge,...  0.86 us
    pallas_call x1, Pallas kernels, per_device(): call(functools.partial(link_kernel, blocks, 2), 'links', (shaped(points *...  0.79 us
  transfers between devices with their start and end apart: 6, of which 4 were waited for; matrix products, arithmetic and copies ran while one was open for 0% of the time, Pallas kernels for 23%

profile of v2, /device:TPU:0, one launch (start us, length us, event | category | flops | bytes accessed | tf_op | source)
XLA Modules:
  0.0 17.5 jit_solution(15474965721861821313)
XLA Ops:
  0.6 0.0 copy-start
  0.6 0.0 copy-start.1
  0.7 0.9 %pack.1.own = f32[104,128]{1,0:T(8,128)S(1)} custom-call(f32[4]{0:T(128)} %storage.1, f32[32,128]{1,0:T(8,128)} %bitcast.16, f32[32,128]{1,0:T(8,128)} %bitcast.17, s32[32,128]{1,0:T(8,128)} %bitcast.18, f32[32,128]{1,0:T(8,128)} %bitcast.19, s32[4,128]{1,0:T(4,128)} %bitcast.20), custom_call_target="tpu_custom_call" | custom-call | flops 1000 | bytes 100000 | tf_op jit(solution)/shard_map/pack/pallas_call | solution.py:561
  1.5 0.5 %collective-permute-start = (f32[104,128]{1,0:T(8,128)S(1)}, f32[104,128]{1,0:T(8,128)S(1)}, u32[]{:S(2)}, u32[]{:S(2)}) collective-permute-start(f32[104,128]{1,0:T(8,128)S(1)} %pack.1.own), channel_id=1, source_target_pairs={{0,2},{1,3},{4,6},{5,7},{8,10},{9,11},{12,14},{13,15},{16,18},{17,... | collective-permute-start | bytes 159752 | tf_op jit(solution)/shard_map/ppermute | solution.py:552
  2.0 0.9 %collective-permute-done.partner = f32[104,128]{1,0:T(8,128)S(1)} collective-permute-done((f32[104,128]{1,0:T(8,128)S(1)}, f32[104,128]{1,0:T(8,128)S(1)}, u32[]{:S(2)}, u32[]{:S(2)}) %collective-permute-start) | collective-permute-done | bytes 53280 | tf_op jit(solution)/shard_map/ppermute | solution.py:552
  2.9 2.9 %collective-permute-start.1 = (f32[208,128]{1,0:T(8,128)S(1)}, f32[208,128]{1,0:T(8,128)S(1)}, u32[]{:S(2)}, u32[]{:S(2)}) collective-permute-start(f32[208,128]{1,0:T(8,128)S(1)} %pad_maximum_fusion), channel_id=1, source_target_pairs={{4,2},{5,3},{8,6},{9,7},{12,10},{13,11},{16,14},{17,15},{20,18},{2... | collective-permute-start | bytes 319496 | tf_op jit(solution)/shard_map/ppermute | solution.py:552
  5.8 0.1 collective-permute-start.2
  5.9 1.4 %columns.1 = (f32[32,80,128]{2,1,0:T(8,128)S(1)}, f32[176,128]{1,0:T(8,128)S(1)}, f32[32,128]{1,0:T(8,128)S(1)}) custom-call(f32[32,32]{1,0:T(8,128)} %weights.1, f32[32,80,128]{2,1,0:T(8,128)} %bitcast.14, f32[80,128]{1,0:T(8,128)} %bitcast.15, f32[40,40]{1,0:T(8,128)} %salt_matrix.1), custom_call_target="tpu_custom_call" | custom-call | flops 10000000 | bytes 3000000 | tf_op jit(solution)/shard_map/columns/pallas_call | solution.py:589
  7.3 2.0 %collective-permute-start.5 = (f32[176,128]{1,0:T(8,128)S(1)}, f32[176,128]{1,0:T(8,128)S(1)}, u32[]{:S(2)}, u32[]{:S(2)}) collective-permute-start(f32[176,128]{1,0:T(8,128)S(1)} %get-tuple-element.31.local), channel_id=1, source_target_pairs={{0,1},{1,0},{2,3},{3,2},{4,5},{5,4},{6,7},{7,6},{8,9},{9,8},{10,11... | collective-permute-start | bytes 270344 | tf_op jit(solution)/shard_map/ppermute | solution.py:552
  9.3 0.4 %collective-permute-done.2.far = f32[64,128]{1,0:T(8,128)S(1)} collective-permute-done((f32[64,128]{1,0:T(8,128)S(1)}, f32[64,128]{1,0:T(8,128)S(1)}, u32[]{:S(2)}, u32[]{:S(2)}) %collective-permute-start.2) | collective-permute-done | bytes 32800 | tf_op jit(solution)/shard_map/ppermute | solution.py:552
  9.8 0.0 collective-permute-done.1.near
  9.8 0.2 %collective-permute-start.3 = (f32[168,128]{1,0:T(8,128)S(1)}, f32[168,128]{1,0:T(8,128)S(1)}, u32[]{:S(2)}, u32[]{:S(2)}) collective-permute-start(f32[168,128]{1,0:T(8,128)S(1)} %slice.7), channel_id=1, source_target_pairs={{0,2},{1,3},{4,6},{5,7},{8,10},{9,11},{12,14},{13,15},{16,18},{17,... | collective-permute-start | bytes 258056 | tf_op jit(solution)/shard_map/ppermute | solution.py:552
  10.0 0.0 copy-done.1
  10.0 0.8 %links.1 = (f32[160,64]{1,0:T(8,128)S(1)}, f32[32,160]{1,0:T(8,128)S(1)}) custom-call(f32[16,40]{1,0:T(8,128)S(1)} %bitcast.13), custom_call_target="tpu_custom_call" | custom-call | flops 1000000 | bytes 100000 | tf_op jit(solution)/shard_map/links/pallas_call | solution.py:620
  10.8 0.3 %collective-permute-done.3.inner = f32[168,128]{1,0:T(8,128)S(1)} collective-permute-done((f32[168,128]{1,0:T(8,128)S(1)}, f32[168,128]{1,0:T(8,128)S(1)}, u32[]{:S(2)}, u32[]{:S(2)}) %collective-permute-start.3) | collective-permute-done | bytes 86048 | tf_op jit(solution)/shard_map/ppermute | solution.py:552
  11.1 0.3 %sweeps.1 = (f32[104,128]{1,0:T(8,128)S(1)}, f32[40,128]{1,0:T(8,128)S(1)}) custom-call(f32[104,128]{1,0:T(8,128)S(1)} %pack.1.own, f32[104,128]{1,0:T(8,128)S(1)} %collective-permute-done.partner, f32[208,128]{1,0:T(8,128)S(1)} %collective-permute-done.1.near, f32[64,128]{1,0:T(8,128)S(1)} %collective-permute-done.2.far, ...), custom_call_target="tpu_custom_call" | custom-call | flops 1000000 | bytes 500000 | tf_op jit(solution)/shard_map/sweeps/pallas_call | solution.py:630
  11.4 1.4 %collective-permute-start.4 = (f32[104,128]{1,0:T(8,128)S(1)}, f32[104,128]{1,0:T(8,128)S(1)}, u32[]{:S(2)}, u32[]{:S(2)}) collective-permute-start(f32[104,128]{1,0:T(8,128)S(1)} %get-tuple-element.30.mine), channel_id=1, source_target_pairs={{0,1},{1,0},{2,3},{3,2},{4,5},{5,4},{6,7},{7,6},{8,9},{9,8},{10,11... | collective-permute-start | bytes 159752 | tf_op jit(solution)/shard_map/ppermute | solution.py:552
  12.8 0.0 collective-permute-done.5.other_local
  12.8 0.0 copy-done
  12.8 1.6 %grains.1.base = f32[32,80,128]{2,1,0:T(8,128)S(1)} custom-call(f32[32,80,128]{2,1,0:T(8,128)S(1)} %get-tuple-element.36.grain, f32[32,32]{1,0:T(8,128)S(1)} %copy-done), custom_call_target="tpu_custom_call" | custom-call | flops 1000000000 | bytes 3000000 | tf_op jit(solution)/shard_map/grains/pallas_call | solution.py:641
  14.3 1.2 %collective-permute-done.4.other = f32[104,128]{1,0:T(8,128)S(1)} collective-permute-done((f32[104,128]{1,0:T(8,128)S(1)}, f32[104,128]{1,0:T(8,128)S(1)}, u32[]{:S(2)}, u32[]{:S(2)}) %collective-permute-start.4) | collective-permute-done | bytes 53280 | tf_op jit(solution)/shard_map/ppermute | solution.py:552
  15.6 1.9 %reaction.1 = (f32[32,128]{1,0:T(8,128)}, f32[32,128]{1,0:T(8,128)}, f32[32,128]{1,0:T(8,128)}, f32[32,80,128]{2,1,0:T(8,128)}, f32[80,128]{1,0:T(8,128)}) custom-call(f32[32,128]{1,0:T(8,128)S(1)} %get-tuple-element.25.factors, f32[104,128]{1,0:T(8,128)S(1)} %get-tuple-element.30.mine, f32[104,128]{1,0:T(8,128)S(1)} %collective-permute-done.4.other, ...), custom_call_target="tpu_custom_call" | custom-call | flops 10000000 | bytes 3000000 | tf_op jit(solution)/shard_map/reaction/pallas_call | solution.py:644
  (3 shorter events, 0.0 us)
Async XLA Ops:
  0.6 12.1 %copy-start = (f32[32,32]{1,0:T(8,128)S(1)}, f32[32,32]{1,0:T(8,128)}, u32[]{:S(2)}) copy-start(f32[32,32]{1,0:T(8,128)} %weights.1) | copy-start | bytes 12292
  0.6 9.4 %copy-start.1 = (f32[40,16]{0,1:T(8,128)S(1)}, f32[40,16]{0,1:T(8,128)}, u32[]{:S(2)}) copy-start(f32[40,16]{0,1:T(8,128)} %param.17) | copy-start | bytes 7684
  1.5 1.4 %collective-permute-start = (f32[104,128]{1,0:T(8,128)S(1)}, f32[104,128]{1,0:T(8,128)S(1)}, u32[]{:S(2)}, u32[]{:S(2)}) collective-permute-start(f32[104,128]{1,0:T(8,128)S(1)} %pack.1.own), channel_id=1, source_target_pairs={{0,2},{1,3},{4,6},{5,7},{8,10},{9,11},{12,14},{13,15},{16,18},{17,... | collective-permute-start | bytes 159752 | tf_op jit(solution)/shard_map/ppermute | solution.py:552
  2.9 6.8 %collective-permute-start.1 = (f32[208,128]{1,0:T(8,128)S(1)}, f32[208,128]{1,0:T(8,128)S(1)}, u32[]{:S(2)}, u32[]{:S(2)}) collective-permute-start(f32[208,128]{1,0:T(8,128)S(1)} %pad_maximum_fusion), channel_id=1, source_target_pairs={{4,2},{5,3},{8,6},{9,7},{12,10},{13,11},{16,14},{17,15},{20,18},{2... | collective-permute-start | bytes 319496 | tf_op jit(solution)/shard_map/ppermute | solution.py:552
  5.8 3.9 %collective-permute-start.2 = (f32[64,128]{1,0:T(8,128)S(1)}, f32[64,128]{1,0:T(8,128)S(1)}, u32[]{:S(2)}, u32[]{:S(2)}) collective-permute-start(f32[64,128]{1,0:T(8,128)S(1)} %slice.8), channel_id=1, source_target_pairs={{8,2},{9,3},{12,6},{13,7},{16,10},{17,11},{20,14},{21,15},{24,18},... | collective-permute-start | bytes 98312 | tf_op jit(solution)/shard_map/ppermute | solution.py:552
  7.3 5.4 %collective-permute-start.5 = (f32[176,128]{1,0:T(8,128)S(1)}, f32[176,128]{1,0:T(8,128)S(1)}, u32[]{:S(2)}, u32[]{:S(2)}) collective-permute-start(f32[176,128]{1,0:T(8,128)S(1)} %get-tuple-element.31.local), channel_id=1, source_target_pairs={{0,1},{1,0},{2,3},{3,2},{4,5},{5,4},{6,7},{7,6},{8,9},{9,8},{10,11... | collective-permute-start | bytes 270344 | tf_op jit(solution)/shard_map/ppermute | solution.py:552
  9.8 1.3 %collective-permute-start.3 = (f32[168,128]{1,0:T(8,128)S(1)}, f32[168,128]{1,0:T(8,128)S(1)}, u32[]{:S(2)}, u32[]{:S(2)}) collective-permute-start(f32[168,128]{1,0:T(8,128)S(1)} %slice.7), channel_id=1, source_target_pairs={{0,2},{1,3},{4,6},{5,7},{8,10},{9,11},{12,14},{13,15},{16,18},{17,... | collective-permute-start | bytes 258056 | tf_op jit(solution)/shard_map/ppermute | solution.py:552
  11.4 4.2 %collective-permute-start.4 = (f32[104,128]{1,0:T(8,128)S(1)}, f32[104,128]{1,0:T(8,128)S(1)}, u32[]{:S(2)}, u32[]{:S(2)}) collective-permute-start(f32[104,128]{1,0:T(8,128)S(1)} %get-tuple-element.30.mine), channel_id=1, source_target_pairs={{0,1},{1,0},{2,3},{3,2},{4,5},{5,4},{6,7},{7,6},{8,9},{9,8},{10,11... | collective-permute-start | bytes 159752 | tf_op jit(solution)/shard_map/ppermute | solution.py:552

commit v3 on v2

--- a/solution.py
+++ b/solution.py
@@ -332,9 +332,10 @@
             base[:, start + k * ROWS : start + (k + 1) * ROWS, :] = part
 
 
-def sweep_kernel(sheets, blocks, tiles, own, partner, near, far, inner, out, masks):
+def sweep_kernel(
+    sheets, blocks, tiles, own, partner, near, skip, far, near_in, skip_in, out, masks
+):
     n = sheets * blocks
-    size = own.shape[0]
     tile = lax.axis_index("tile")
     block = lax.axis_index("layer")
     first = jnp.logical_or(tile == 0, tile == tiles - 1)
@@ -350,15 +351,15 @@
 
     def window(start, rows):
         return [
-            load(near, size + start, rows, keep_outer),
+            load(skip_in, start, rows, keep_outer),
             load(near, start, rows, keep_outer),
             load(own, start, rows),
             load(partner, start, rows),
-            load(inner, start, rows, keep_inner),
+            load(near_in, start, rows, keep_inner),
         ]
 
-    warmth = [load(far, 0, n, keep_far)] + window(0, n) + [load(inner, size, n, keep_inner)]
-    volt = [load(far, n, n, keep_far)] + window(n, n) + [load(inner, size + n, n, keep_inner)]
+    warmth = [load(far, 0, n, keep_far)] + window(0, n) + [load(skip, 0, n, keep_inner)]
+    volt = [load(far, n, n, keep_far)] + window(n, n) + [load(skip, n, n, keep_inner)]
     slope = window(2 * n, n)
     free = window(3 * n, 2 * blocks)
     for i in range(5):
@@ -556,6 +557,8 @@
     beside = beside + across([0, tiles - 1])
     beyond = both_layers(mutual([(t, t - 3) for t in range(4, tiles, 2)]))
     beyond = beyond + across([0, 2, tiles - 3, tiles - 1])
+    skipping = both_layers(mutual([(t, t + 3) for t in range(0, tiles - 3, 2)]))
+    skipping = skipping + across([1, tiles - 2])
     layers = across(range(tiles))
 
     own = call(
@@ -584,14 +587,15 @@
         )
     )
     partner = send(own, cores)
-    near = send(jnp.concatenate([own, partner], axis=0), beside)
+    near = send(own, beside)
+    skip = send(own, skipping)
     far = send(own[0 : 2 * n], beyond)
     held, local, factors = call(
         local_kernel,
         "columns",
         (
             shaped(shells, nodes, LANES),
-            shaped(2 * nodes + 2 * ROWS, LANES),
+            shaped(2 * nodes, LANES),
             shaped(shells, LANES),
         ),
         [HBM] * 4,
@@ -614,9 +618,20 @@
         )
     )
     other_local = send(local, layers)
-    near, far, held, local, turned = lax.optimization_barrier(
-        (near, far, held, local, sheet_node_link_matrix.T)
-    )
+    near_in = send(near, cores)
+    near, skip, far, held, local = lax.optimization_barrier((near, skip, far, held, local))
+    skip_in = send(skip, cores)
+    mine, masks = call(
+        functools.partial(sweep_kernel, sheets, blocks, tiles),
+        "sweeps",
+        (shaped(2 * n + 5 * edge, LANES), shaped(5 * edge, LANES)),
+        [VMEM] * 7,
+        (VMEM, VMEM),
+        10**6,
+        500000,
+    )(own, partner, near, skip, far, near_in, skip_in)
+    other = send(mine, layers)
+    masks, turned = lax.optimization_barrier((masks, sheet_node_link_matrix.T))
     link, turned = call(
         functools.partial(link_kernel, blocks, 2),
         "links",
@@ -626,17 +641,6 @@
         10**6,
         100000,
     )(turned)
-    inner = send(near[0 : size + 2 * n], cores)
-    mine, masks = call(
-        functools.partial(sweep_kernel, sheets, blocks, tiles),
-        "sweeps",
-        (shaped(2 * n + 5 * edge, LANES), shaped(5 * edge, LANES)),
-        [VMEM] * 5,
-        (VMEM, VMEM),
-        10**6,
-        500000,
-    )(own, partner, near, far, inner)
-    other = send(mine, layers)
     held, masks, other_local = lax.optimization_barrier((held, masks, other_local))
     base = call(
         grain_kernel, "grains", shaped(shells, nodes, LANES), [VMEM] * 2, VMEM, 10**9, 3000000

time: 17.7 us -> 17.4 us (0.983)
  waiting for transfers between devices: 2.84 us -> 2.11 us
  starting transfers between devices: 7.14 us -> 7.59 us
    ppermute x6 -> x8, waiting for transfers between devices: 2.84 us -> 2.11 us  [send(): return lax.ppermute(value, ('tile', 'layer'), pairs)]
    ppermute x6 -> x8, starting transfers between devices: 7.14 us -> 7.59 us  [send(): return lax.ppermute(value, ('tile', 'layer'), pairs)]
  transfers between devices with their start and end apart: 6 -> 8, of which waited for: 4 -> 5; matrix products, arithmetic and copies ran while one was open for 0% -> 0% of each run, Pallas kernels for 23% -> 23%
where the time goes in v3:
time: 17.4 us; the launch traced here: 17.2 us
  starting transfers between devices  7.59 us (44%)
  Pallas kernels  6.74 us (39%)
  waiting for transfers between devices  2.11 us (12%)
  between operations  0.71 us (4%)
    ppermute x8, starting transfers between devices, send(): return lax.ppermute(value, ('tile', 'layer'), pairs)  7.59 us
    ppermute x8, waiting for transfers between devices, send(): return lax.ppermute(value, ('tile', 'layer'), pairs)  2.11 us
    pallas_call x1, Pallas kernels, per_device(): call(functools.partial(reaction_kernel, sheets, blocks), 'reaction', (sha...  1.89 us
    pallas_call x1, Pallas kernels, per_device(): call(grain_kernel, 'grains', shaped(shells, nodes, LANES), [VMEM] * 2, VM...  1.55 us
    pallas_call x1, Pallas kernels, per_device(): call(local_kernel, 'columns', (shaped(shells, nodes, LANES), shaped(2 * n...  1.4 us
    pallas_call x1, Pallas kernels, per_device(): call(functools.partial(pack_kernel, blocks), 'pack', shaped(3 * n + edge,...  0.86 us
    pallas_call x1, Pallas kernels, per_device(): call(functools.partial(link_kernel, blocks, 2), 'links', (shaped(points *...  0.79 us
  transfers between devices with their start and end apart: 8, of which 5 were waited for; matrix products, arithmetic and copies ran while one was open for 0% of the time, Pallas kernels for 23%

profile of v3, /device:TPU:0, one launch (start us, length us, event | category | flops | bytes accessed | tf_op | source)
XLA Modules:
  0.0 17.2 jit_solution(12257377397897262941)
XLA Ops:
  0.6 0.0 copy-start
  0.6 0.0 copy-start.1
  0.7 0.9 %pack.1.own = f32[104,128]{1,0:T(8,128)S(1)} custom-call(f32[4]{0:T(128)} %storage.1, f32[32,128]{1,0:T(8,128)} %bitcast.16, f32[32,128]{1,0:T(8,128)} %bitcast.17, s32[32,128]{1,0:T(8,128)} %bitcast.18, f32[32,128]{1,0:T(8,128)} %bitcast.19, s32[4,128]{1,0:T(4,128)} %bitcast.20), custom_call_target="tpu_custom_call" | custom-call | flops 1000 | bytes 100000 | tf_op jit(solution)/shard_map/pack/pallas_call | solution.py:564
  1.5 2.5 %collective-permute-start.2 = (f32[104,128]{1,0:T(8,128)S(1)}, f32[104,128]{1,0:T(8,128)S(1)}, u32[]{:S(2)}, u32[]{:S(2)}) collective-permute-start(f32[104,128]{1,0:T(8,128)S(1)} %pack.1.own), channel_id=1, source_target_pairs={{0,6},{1,7},{4,10},{5,11},{8,14},{9,15},{12,18},{13,19},{16,22},{1... | collective-permute-start | bytes 159752 | tf_op jit(solution)/shard_map/ppermute | solution.py:553
  4.0 1.5 %collective-permute-start.1 = (f32[104,128]{1,0:T(8,128)S(1)}, f32[104,128]{1,0:T(8,128)S(1)}, u32[]{:S(2)}, u32[]{:S(2)}) collective-permute-start(f32[104,128]{1,0:T(8,128)S(1)} %pack.1.own), channel_id=1, source_target_pairs={{4,2},{5,3},{8,6},{9,7},{12,10},{13,11},{16,14},{17,15},{20,18},{2... | collective-permute-start | bytes 159752 | tf_op jit(solution)/shard_map/ppermute | solution.py:553
  5.5 0.5 %collective-permute-start.3 = (f32[64,128]{1,0:T(8,128)S(1)}, f32[64,128]{1,0:T(8,128)S(1)}, u32[]{:S(2)}, u32[]{:S(2)}) collective-permute-start(f32[64,128]{1,0:T(8,128)S(1)} %slice.4), channel_id=1, source_target_pairs={{8,2},{9,3},{12,6},{13,7},{16,10},{17,11},{20,14},{21,15},{24,18},... | collective-permute-start | bytes 98312 | tf_op jit(solution)/shard_map/ppermute | solution.py:553
  6.0 1.4 %columns.1 = (f32[32,80,128]{2,1,0:T(8,128)S(1)}, f32[160,128]{1,0:T(8,128)S(1)}, f32[32,128]{1,0:T(8,128)S(1)}) custom-call(f32[32,32]{1,0:T(8,128)} %weights.1, f32[32,80,128]{2,1,0:T(8,128)} %bitcast.14, f32[80,128]{1,0:T(8,128)} %bitcast.15, f32[40,40]{1,0:T(8,128)} %salt_matrix.1), custom_call_target="tpu_custom_call" | custom-call | flops 10000000 | bytes 3000000 | tf_op jit(solution)/shard_map/columns/pallas_call | solution.py:593
  7.4 1.6 %collective-permute-start.7 = (f32[160,128]{1,0:T(8,128)S(1)}, f32[160,128]{1,0:T(8,128)S(1)}, u32[]{:S(2)}, u32[]{:S(2)}) collective-permute-start(f32[160,128]{1,0:T(8,128)S(1)} %get-tuple-element.34.local), channel_id=1, source_target_pairs={{0,1},{1,0},{2,3},{3,2},{4,5},{5,4},{6,7},{7,6},{8,9},{9,8},{10,11... | collective-permute-start | bytes 245768 | tf_op jit(solution)/shard_map/ppermute | solution.py:553
  9.0 0.1 collective-permute-start
  9.1 0.4 %collective-permute-done.3.far = f32[64,128]{1,0:T(8,128)S(1)} collective-permute-done((f32[64,128]{1,0:T(8,128)S(1)}, f32[64,128]{1,0:T(8,128)S(1)}, u32[]{:S(2)}, u32[]{:S(2)}) %collective-permute-start.3) | collective-permute-done | bytes 32800 | tf_op jit(solution)/shard_map/ppermute | solution.py:553
  9.4 0.0 collective-permute-done.2.skip
  9.4 0.0 collective-permute-done.1.near
  9.4 0.2 collective-permute-start.4
  9.6 0.3 %collective-permute-start.5 = (f32[104,128]{1,0:T(8,128)S(1)}, f32[104,128]{1,0:T(8,128)S(1)}, u32[]{:S(2)}, u32[]{:S(2)}) collective-permute-start(f32[104,128]{1,0:T(8,128)S(1)} %collective-permute-done.2.skip), channel_id=1, source_target_pairs={{0,2},{1,3},{4,6},{5,7},{8,10},{9,11},{12,14},{13,15},{16,18},{17,... | collective-permute-start | bytes 159752 | tf_op jit(solution)/shard_map/ppermute | solution.py:553
  9.9 0.3 %collective-permute-done.partner = f32[104,128]{1,0:T(8,128)S(1)} collective-permute-done((f32[104,128]{1,0:T(8,128)S(1)}, f32[104,128]{1,0:T(8,128)S(1)}, u32[]{:S(2)}, u32[]{:S(2)}) %collective-permute-start) | collective-permute-done | bytes 53280 | tf_op jit(solution)/shard_map/ppermute | solution.py:553
  10.2 0.4 %collective-permute-done.4.near_in = f32[104,128]{1,0:T(8,128)S(1)} collective-permute-done((f32[104,128]{1,0:T(8,128)S(1)}, f32[104,128]{1,0:T(8,128)S(1)}, u32[]{:S(2)}, u32[]{:S(2)}) %collective-permute-start.4) | collective-permute-done | bytes 53280 | tf_op jit(solution)/shard_map/ppermute | solution.py:553
  10.7 0.2 collective-permute-done.5.skip_in
  10.8 0.2 %sweeps.1 = (f32[104,128]{1,0:T(8,128)S(1)}, f32[40,128]{1,0:T(8,128)S(1)}) custom-call(f32[104,128]{1,0:T(8,128)S(1)} %pack.1.own, f32[104,128]{1,0:T(8,128)S(1)} %collective-permute-done.partner, f32[104,128]{1,0:T(8,128)S(1)} %collective-permute-done.1.near, f32[104,128]{1,0:T(8,128)S(1)} %collective-permute-done.2.skip, ...), custom_call_target="tpu_custom_call" | custom-call | flops 1000000 | bytes 500000 | tf_op jit(solution)/shard_map/sweeps/pallas_call | solution.py:624
  11.1 1.0 %collective-permute-start.6 = (f32[104,128]{1,0:T(8,128)S(1)}, f32[104,128]{1,0:T(8,128)S(1)}, u32[]{:S(2)}, u32[]{:S(2)}) collective-permute-start(f32[104,128]{1,0:T(8,128)S(1)} %get-tuple-element.33.mine), channel_id=1, source_target_pairs={{0,1},{1,0},{2,3},{3,2},{4,5},{5,4},{6,7},{7,6},{8,9},{9,8},{10,11... | collective-permute-start | bytes 159752 | tf_op jit(solution)/shard_map/ppermute | solution.py:553
  12.0 0.0 collective-permute-done.7.other_local
  12.0 0.0 copy-done.1
  12.0 0.8 %links.1 = (f32[160,64]{1,0:T(8,128)S(1)}, f32[32,160]{1,0:T(8,128)S(1)}) custom-call(f32[16,40]{1,0:T(8,128)S(1)} %bitcast.13), custom_call_target="tpu_custom_call" | custom-call | flops 1000000 | bytes 100000 | tf_op jit(solution)/shard_map/links/pallas_call | solution.py:635
  12.9 0.0 copy-done
  12.9 1.5 %grains.1.base = f32[32,80,128]{2,1,0:T(8,128)S(1)} custom-call(f32[32,80,128]{2,1,0:T(8,128)S(1)} %get-tuple-element.40.grain, f32[32,32]{1,0:T(8,128)S(1)} %copy-done), custom_call_target="tpu_custom_call" | custom-call | flops 1000000000 | bytes 3000000 | tf_op jit(solution)/shard_map/grains/pallas_call | solution.py:645
  14.4 0.9 %collective-permute-done.6.other = f32[104,128]{1,0:T(8,128)S(1)} collective-permute-done((f32[104,128]{1,0:T(8,128)S(1)}, f32[104,128]{1,0:T(8,128)S(1)}, u32[]{:S(2)}, u32[]{:S(2)}) %collective-permute-start.6) | collective-permute-done | bytes 53280 | tf_op jit(solution)/shard_map/ppermute | solution.py:553
  15.3 1.9 %reaction.1 = (f32[32,128]{1,0:T(8,128)}, f32[32,128]{1,0:T(8,128)}, f32[32,128]{1,0:T(8,128)}, f32[32,80,128]{2,1,0:T(8,128)}, f32[80,128]{1,0:T(8,128)}) custom-call(f32[32,128]{1,0:T(8,128)S(1)} %get-tuple-element.27.factors, f32[104,128]{1,0:T(8,128)S(1)} %get-tuple-element.33.mine, f32[104,128]{1,0:T(8,128)S(1)} %collective-permute-done.6.other, ...), custom_call_target="tpu_custom_call" | custom-call | flops 10000000 | bytes 3000000 | tf_op jit(solution)/shard_map/reaction/pallas_call | solution.py:648
  (1 shorter events, 0.0 us)
Async XLA Ops:
  0.6 12.2 %copy-start = (f32[32,32]{1,0:T(8,128)S(1)}, f32[32,32]{1,0:T(8,128)}, u32[]{:S(2)}) copy-start(f32[32,32]{1,0:T(8,128)} %weights.1) | copy-start | bytes 12292
  0.6 11.4 %copy-start.1 = (f32[40,16]{0,1:T(8,128)S(1)}, f32[40,16]{0,1:T(8,128)}, u32[]{:S(2)}) copy-start(f32[40,16]{0,1:T(8,128)} %param.17) | copy-start | bytes 7684
  1.5 7.9 %collective-permute-start.2 = (f32[104,128]{1,0:T(8,128)S(1)}, f32[104,128]{1,0:T(8,128)S(1)}, u32[]{:S(2)}, u32[]{:S(2)}) collective-permute-start(f32[104,128]{1,0:T(8,128)S(1)} %pack.1.own), channel_id=1, source_target_pairs={{0,6},{1,7},{4,10},{5,11},{8,14},{9,15},{12,18},{13,19},{16,22},{1... | collective-permute-start | bytes 159752 | tf_op jit(solution)/shard_map/ppermute | solution.py:553
  4.0 5.4 %collective-permute-start.1 = (f32[104,128]{1,0:T(8,128)S(1)}, f32[104,128]{1,0:T(8,128)S(1)}, u32[]{:S(2)}, u32[]{:S(2)}) collective-permute-start(f32[104,128]{1,0:T(8,128)S(1)} %pack.1.own), channel_id=1, source_target_pairs={{4,2},{5,3},{8,6},{9,7},{12,10},{13,11},{16,14},{17,15},{20,18},{2... | collective-permute-start | bytes 159752 | tf_op jit(solution)/shard_map/ppermute | solution.py:553
  5.5 3.9 %collective-permute-start.3 = (f32[64,128]{1,0:T(8,128)S(1)}, f32[64,128]{1,0:T(8,128)S(1)}, u32[]{:S(2)}, u32[]{:S(2)}) collective-permute-start(f32[64,128]{1,0:T(8,128)S(1)} %slice.4), channel_id=1, source_target_pairs={{8,2},{9,3},{12,6},{13,7},{16,10},{17,11},{20,14},{21,15},{24,18},... | collective-permute-start | bytes 98312 | tf_op jit(solution)/shard_map/ppermute | solution.py:553
  7.4 4.6 %collective-permute-start.7 = (f32[160,128]{1,0:T(8,128)S(1)}, f32[160,128]{1,0:T(8,128)S(1)}, u32[]{:S(2)}, u32[]{:S(2)}) collective-permute-start(f32[160,128]{1,0:T(8,128)S(1)} %get-tuple-element.34.local), channel_id=1, source_target_pairs={{0,1},{1,0},{2,3},{3,2},{4,5},{5,4},{6,7},{7,6},{8,9},{9,8},{10,11... | collective-permute-start | bytes 245768 | tf_op jit(solution)/shard_map/ppermute | solution.py:553
  9.0 1.2 %collective-permute-start = (f32[104,128]{1,0:T(8,128)S(1)}, f32[104,128]{1,0:T(8,128)S(1)}, u32[]{:S(2)}, u32[]{:S(2)}) collective-permute-start(f32[104,128]{1,0:T(8,128)S(1)} %pack.1.own), channel_id=1, source_target_pairs={{0,2},{1,3},{4,6},{5,7},{8,10},{9,11},{12,14},{13,15},{16,18},{17,... | collective-permute-start | bytes 159752 | tf_op jit(solution)/shard_map/ppermute | solution.py:553
  9.4 1.2 %collective-permute-start.4 = (f32[104,128]{1,0:T(8,128)S(1)}, f32[104,128]{1,0:T(8,128)S(1)}, u32[]{:S(2)}, u32[]{:S(2)}) collective-permute-start(f32[104,128]{1,0:T(8,128)S(1)} %collective-permute-done.1.near), channel_id=1, source_target_pairs={{0,2},{1,3},{4,6},{5,7},{8,10},{9,11},{12,14},{13,15},{16,18},{17,... | collective-permute-start | bytes 159752 | tf_op jit(solution)/shard_map/ppermute | solution.py:553
  9.6 1.2 %collective-permute-start.5 = (f32[104,128]{1,0:T(8,128)S(1)}, f32[104,128]{1,0:T(8,128)S(1)}, u32[]{:S(2)}, u32[]{:S(2)}) collective-permute-start(f32[104,128]{1,0:T(8,128)S(1)} %collective-permute-done.2.skip), channel_id=1, source_target_pairs={{0,2},{1,3},{4,6},{5,7},{8,10},{9,11},{12,14},{13,15},{16,18},{17,... | collective-permute-start | bytes 159752 | tf_op jit(solution)/shard_map/ppermute | solution.py:553
  11.1 4.2 %collective-permute-start.6 = (f32[104,128]{1,0:T(8,128)S(1)}, f32[104,128]{1,0:T(8,128)S(1)}, u32[]{:S(2)}, u32[]{:S(2)}) collective-permute-start(f32[104,128]{1,0:T(8,128)S(1)} %get-tuple-element.33.mine), channel_id=1, source_target_pairs={{0,1},{1,0},{2,3},{3,2},{4,5},{5,4},{6,7},{7,6},{8,9},{9,8},{10,11... | collective-permute-start | bytes 159752 | tf_op jit(solution)/shard_map/ppermute | solution.py:553

commit v4 on v3

--- a/solution.py
+++ b/solution.py
@@ -434,8 +434,8 @@
     for i in range(5):
         at = 2 * n + i * edge
         added.append(pltpu.roll(mine[at : at + edge, :], blocks, 0) * other[at : at + edge, :])
-    volt = [jnp.zeros_like(added[0])] * 7
-    for sweep in range(SWEEPS):
+    volt = [free[i] * (imposed_excitation * added[i]) for i in range(5)]
+    for sweep in range(1, SWEEPS):
         volt = [
             free[i + sweep]
             * (
@@ -465,9 +465,12 @@
     salt = jnp.concatenate(
         [local[nodes : 2 * nodes, :], other_local[nodes : 2 * nodes, :]], axis=0
     )
-    rate = 1.0 / ((1.0 + jnp.exp(-0.3 * node[:, 0:LANES])) * (1.0 + jnp.exp(-salt)))
+    rate = (1.0 / (1.0 + jnp.exp(-0.3 * node[:, 0:LANES]))) * (1.0 / (1.0 + jnp.exp(-salt)))
     reaction, source = react(surface_base, gain, rate, node[:, LANES:])
-    sheets_now[...] = dot(turned[...], jnp.concatenate([source, reaction], axis=1))
+    link_high, link_low = halves(turned[...])
+    high, low = halves(jnp.concatenate([source, reaction], axis=1))
+    short = functools.partial(jnp.dot, preferred_element_type=jnp.float32)
+    sheets_now[...] = short(link_high, high) + (short(link_high, low) + short(link_low, high))
     late = [
         pltpu.make_async_copy(sheets_now.at[:, 0:LANES], warming, sems.at[2]),
         pltpu.make_async_copy(sheets_now.at[:, LANES:], flux, sems.at[3]),

time: 17.4 us -> 17.3 us (level)
  no operation moved by 1% of the time
where the time goes in v4:
time: 17.3 us; the launch traced here: 17.1 us
  starting transfers between devices  7.59 us (44%)
  Pallas kernels  6.63 us (38%)
  waiting for transfers between devices  2.11 us (12%)
  between operations  0.71 us (4%)
    ppermute x8, starting transfers between devices, send(): return lax.ppermute(value, ('tile', 'layer'), pairs)  7.59 us
    ppermute x8, waiting for transfers between devices, send(): return lax.ppermute(value, ('tile', 'layer'), pairs)  2.11 us
    pallas_call x1, Pallas kernels, per_device(): call(functools.partial(reaction_kernel, sheets, blocks), 'reaction', (sha...  1.78 us
    pallas_call x1, Pallas kernels, per_device(): call(grain_kernel, 'grains', shaped(shells, nodes, LANES), [VMEM] * 2, VM...  1.55 us
    pallas_call x1, Pallas kernels, per_device(): call(local_kernel, 'columns', (shaped(shells, nodes, LANES), shaped(2 * n...  1.4 us
    pallas_call x1, Pallas kernels, per_device(): call(functools.partial(pack_kernel, blocks), 'pack', shaped(3 * n + edge,...  0.86 us
    pallas_call x1, Pallas kernels, per_device(): call(functools.partial(link_kernel, blocks, 2), 'links', (shaped(points *...  0.79 us
  transfers between devices with their start and end apart: 8, of which 5 were waited for; matrix products, arithmetic and copies ran while one was open for 0% of the time, Pallas kernels for 23%

profile of v4, /device:TPU:0, one launch (start us, length us, event | category | flops | bytes accessed | tf_op | source)
XLA Modules:
  0.0 17.1 jit_solution(2889244066739510476)
XLA Ops:
  0.6 0.0 copy-start
  0.6 0.0 copy-start.1
  0.7 0.9 %pack.1.own = f32[104,128]{1,0:T(8,128)S(1)} custom-call(f32[4]{0:T(128)} %storage.1, f32[32,128]{1,0:T(8,128)} %bitcast.16, f32[32,128]{1,0:T(8,128)} %bitcast.17, s32[32,128]{1,0:T(8,128)} %bitcast.18, f32[32,128]{1,0:T(8,128)} %bitcast.19, s32[4,128]{1,0:T(4,128)} %bitcast.20), custom_call_target="tpu_custom_call" | custom-call | flops 1000 | bytes 100000 | tf_op jit(solution)/shard_map/pack/pallas_call | solution.py:567
  1.5 2.5 %collective-permute-start.2 = (f32[104,128]{1,0:T(8,128)S(1)}, f32[104,128]{1,0:T(8,128)S(1)}, u32[]{:S(2)}, u32[]{:S(2)}) collective-permute-start(f32[104,128]{1,0:T(8,128)S(1)} %pack.1.own), channel_id=1, source_target_pairs={{0,6},{1,7},{4,10},{5,11},{8,14},{9,15},{12,18},{13,19},{16,22},{1... | collective-permute-start | bytes 159752 | tf_op jit(solution)/shard_map/ppermute | solution.py:556
  4.0 1.5 %collective-permute-start.1 = (f32[104,128]{1,0:T(8,128)S(1)}, f32[104,128]{1,0:T(8,128)S(1)}, u32[]{:S(2)}, u32[]{:S(2)}) collective-permute-start(f32[104,128]{1,0:T(8,128)S(1)} %pack.1.own), channel_id=1, source_target_pairs={{4,2},{5,3},{8,6},{9,7},{12,10},{13,11},{16,14},{17,15},{20,18},{2... | collective-permute-start | bytes 159752 | tf_op jit(solution)/shard_map/ppermute | solution.py:556
  5.5 0.5 %collective-permute-start.3 = (f32[64,128]{1,0:T(8,128)S(1)}, f32[64,128]{1,0:T(8,128)S(1)}, u32[]{:S(2)}, u32[]{:S(2)}) collective-permute-start(f32[64,128]{1,0:T(8,128)S(1)} %slice.4), channel_id=1, source_target_pairs={{8,2},{9,3},{12,6},{13,7},{16,10},{17,11},{20,14},{21,15},{24,18},... | collective-permute-start | bytes 98312 | tf_op jit(solution)/shard_map/ppermute | solution.py:556
  6.0 1.4 %columns.1 = (f32[32,80,128]{2,1,0:T(8,128)S(1)}, f32[160,128]{1,0:T(8,128)S(1)}, f32[32,128]{1,0:T(8,128)S(1)}) custom-call(f32[32,32]{1,0:T(8,128)} %weights.1, f32[32,80,128]{2,1,0:T(8,128)} %bitcast.14, f32[80,128]{1,0:T(8,128)} %bitcast.15, f32[40,40]{1,0:T(8,128)} %salt_matrix.1), custom_call_target="tpu_custom_call" | custom-call | flops 10000000 | bytes 3000000 | tf_op jit(solution)/shard_map/columns/pallas_call | solution.py:596
  7.4 1.6 %collective-permute-start.7 = (f32[160,128]{1,0:T(8,128)S(1)}, f32[160,128]{1,0:T(8,128)S(1)}, u32[]{:S(2)}, u32[]{:S(2)}) collective-permute-start(f32[160,128]{1,0:T(8,128)S(1)} %get-tuple-element.34.local), channel_id=1, source_target_pairs={{0,1},{1,0},{2,3},{3,2},{4,5},{5,4},{6,7},{7,6},{8,9},{9,8},{10,11... | collective-permute-start | bytes 245768 | tf_op jit(solution)/shard_map/ppermute | solution.py:556
  9.0 0.1 collective-permute-start
  9.1 0.4 %collective-permute-done.3.far = f32[64,128]{1,0:T(8,128)S(1)} collective-permute-done((f32[64,128]{1,0:T(8,128)S(1)}, f32[64,128]{1,0:T(8,128)S(1)}, u32[]{:S(2)}, u32[]{:S(2)}) %collective-permute-start.3) | collective-permute-done | bytes 32800 | tf_op jit(solution)/shard_map/ppermute | solution.py:556
  9.4 0.0 collective-permute-done.2.skip
  9.4 0.0 collective-permute-done.1.near
  9.4 0.2 collective-permute-start.4
  9.6 0.3 %collective-permute-start.5 = (f32[104,128]{1,0:T(8,128)S(1)}, f32[104,128]{1,0:T(8,128)S(1)}, u32[]{:S(2)}, u32[]{:S(2)}) collective-permute-start(f32[104,128]{1,0:T(8,128)S(1)} %collective-permute-done.2.skip), channel_id=1, source_target_pairs={{0,2},{1,3},{4,6},{5,7},{8,10},{9,11},{12,14},{13,15},{16,18},{17,... | collective-permute-start | bytes 159752 | tf_op jit(solution)/shard_map/ppermute | solution.py:556
  9.9 0.3 %collective-permute-done.partner = f32[104,128]{1,0:T(8,128)S(1)} collective-permute-done((f32[104,128]{1,0:T(8,128)S(1)}, f32[104,128]{1,0:T(8,128)S(1)}, u32[]{:S(2)}, u32[]{:S(2)}) %collective-permute-start) | collective-permute-done | bytes 53280 | tf_op jit(solution)/shard_map/ppermute | solution.py:556
  10.2 0.4 %collective-permute-done.4.near_in = f32[104,128]{1,0:T(8,128)S(1)} collective-permute-done((f32[104,128]{1,0:T(8,128)S(1)}, f32[104,128]{1,0:T(8,128)S(1)}, u32[]{:S(2)}, u32[]{:S(2)}) %collective-permute-start.4) | collective-permute-done | bytes 53280 | tf_op jit(solution)/shard_map/ppermute | solution.py:556
  10.7 0.2 collective-permute-done.5.skip_in
  10.8 0.2 %sweeps.1 = (f32[104,128]{1,0:T(8,128)S(1)}, f32[40,128]{1,0:T(8,128)S(1)}) custom-call(f32[104,128]{1,0:T(8,128)S(1)} %pack.1.own, f32[104,128]{1,0:T(8,128)S(1)} %collective-permute-done.partner, f32[104,128]{1,0:T(8,128)S(1)} %collective-permute-done.1.near, f32[104,128]{1,0:T(8,128)S(1)} %collective-permute-done.2.skip, ...), custom_call_target="tpu_custom_call" | custom-call | flops 1000000 | bytes 500000 | tf_op jit(solution)/shard_map/sweeps/pallas_call | solution.py:627
  11.1 1.0 %collective-permute-start.6 = (f32[104,128]{1,0:T(8,128)S(1)}, f32[104,128]{1,0:T(8,128)S(1)}, u32[]{:S(2)}, u32[]{:S(2)}) collective-permute-start(f32[104,128]{1,0:T(8,128)S(1)} %get-tuple-element.33.mine), channel_id=1, source_target_pairs={{0,1},{1,0},{2,3},{3,2},{4,5},{5,4},{6,7},{7,6},{8,9},{9,8},{10,11... | collective-permute-start | bytes 159752 | tf_op jit(solution)/shard_map/ppermute | solution.py:556
  12.0 0.0 collective-permute-done.7.other_local
  12.0 0.0 copy-done.1
  12.0 0.8 %links.1 = (f32[160,64]{1,0:T(8,128)S(1)}, f32[32,160]{1,0:T(8,128)S(1)}) custom-call(f32[16,40]{1,0:T(8,128)S(1)} %bitcast.13), custom_call_target="tpu_custom_call" | custom-call | flops 1000000 | bytes 100000 | tf_op jit(solution)/shard_map/links/pallas_call | solution.py:638
  12.9 0.0 copy-done
  12.9 1.5 %grains.1.base = f32[32,80,128]{2,1,0:T(8,128)S(1)} custom-call(f32[32,80,128]{2,1,0:T(8,128)S(1)} %get-tuple-element.40.grain, f32[32,32]{1,0:T(8,128)S(1)} %copy-done), custom_call_target="tpu_custom_call" | custom-call | flops 1000000000 | bytes 3000000 | tf_op jit(solution)/shard_map/grains/pallas_call | solution.py:648
  14.4 0.9 %collective-permute-done.6.other = f32[104,128]{1,0:T(8,128)S(1)} collective-permute-done((f32[104,128]{1,0:T(8,128)S(1)}, f32[104,128]{1,0:T(8,128)S(1)}, u32[]{:S(2)}, u32[]{:S(2)}) %collective-permute-start.6) | collective-permute-done | bytes 53280 | tf_op jit(solution)/shard_map/ppermute | solution.py:556
  15.3 1.8 %reaction.1 = (f32[32,128]{1,0:T(8,128)}, f32[32,128]{1,0:T(8,128)}, f32[32,128]{1,0:T(8,128)}, f32[32,80,128]{2,1,0:T(8,128)}, f32[80,128]{1,0:T(8,128)}) custom-call(f32[32,128]{1,0:T(8,128)S(1)} %get-tuple-element.27.factors, f32[104,128]{1,0:T(8,128)S(1)} %get-tuple-element.33.mine, f32[104,128]{1,0:T(8,128)S(1)} %collective-permute-done.6.other, ...), custom_call_target="tpu_custom_call" | custom-call | flops 10000000 | bytes 3000000 | tf_op jit(solution)/shard_map/reaction/pallas_call | solution.py:651
  (1 shorter events, 0.0 us)
Async XLA Ops:
  0.6 12.2 %copy-start = (f32[32,32]{1,0:T(8,128)S(1)}, f32[32,32]{1,0:T(8,128)}, u32[]{:S(2)}) copy-start(f32[32,32]{1,0:T(8,128)} %weights.1) | copy-start | bytes 12292
  0.6 11.4 %copy-start.1 = (f32[40,16]{0,1:T(8,128)S(1)}, f32[40,16]{0,1:T(8,128)}, u32[]{:S(2)}) copy-start(f32[40,16]{0,1:T(8,128)} %param.17) | copy-start | bytes 7684
  1.5 7.9 %collective-permute-start.2 = (f32[104,128]{1,0:T(8,128)S(1)}, f32[104,128]{1,0:T(8,128)S(1)}, u32[]{:S(2)}, u32[]{:S(2)}) collective-permute-start(f32[104,128]{1,0:T(8,128)S(1)} %pack.1.own), channel_id=1, source_target_pairs={{0,6},{1,7},{4,10},{5,11},{8,14},{9,15},{12,18},{13,19},{16,22},{1... | collective-permute-start | bytes 159752 | tf_op jit(solution)/shard_map/ppermute | solution.py:556
  4.0 5.4 %collective-permute-start.1 = (f32[104,128]{1,0:T(8,128)S(1)}, f32[104,128]{1,0:T(8,128)S(1)}, u32[]{:S(2)}, u32[]{:S(2)}) collective-permute-start(f32[104,128]{1,0:T(8,128)S(1)} %pack.1.own), channel_id=1, source_target_pairs={{4,2},{5,3},{8,6},{9,7},{12,10},{13,11},{16,14},{17,15},{20,18},{2... | collective-permute-start | bytes 159752 | tf_op jit(solution)/shard_map/ppermute | solution.py:556
  5.5 3.9 %collective-permute-start.3 = (f32[64,128]{1,0:T(8,128)S(1)}, f32[64,128]{1,0:T(8,128)S(1)}, u32[]{:S(2)}, u32[]{:S(2)}) collective-permute-start(f32[64,128]{1,0:T(8,128)S(1)} %slice.4), channel_id=1, source_target_pairs={{8,2},{9,3},{12,6},{13,7},{16,10},{17,11},{20,14},{21,15},{24,18},... | collective-permute-start | bytes 98312 | tf_op jit(solution)/shard_map/ppermute | solution.py:556
  7.4 4.6 %collective-permute-start.7 = (f32[160,128]{1,0:T(8,128)S(1)}, f32[160,128]{1,0:T(8,128)S(1)}, u32[]{:S(2)}, u32[]{:S(2)}) collective-permute-start(f32[160,128]{1,0:T(8,128)S(1)} %get-tuple-element.34.local), channel_id=1, source_target_pairs={{0,1},{1,0},{2,3},{3,2},{4,5},{5,4},{6,7},{7,6},{8,9},{9,8},{10,11... | collective-permute-start | bytes 245768 | tf_op jit(solution)/shard_map/ppermute | solution.py:556
  9.0 1.2 %collective-permute-start = (f32[104,128]{1,0:T(8,128)S(1)}, f32[104,128]{1,0:T(8,128)S(1)}, u32[]{:S(2)}, u32[]{:S(2)}) collective-permute-start(f32[104,128]{1,0:T(8,128)S(1)} %pack.1.own), channel_id=1, source_target_pairs={{0,2},{1,3},{4,6},{5,7},{8,10},{9,11},{12,14},{13,15},{16,18},{17,... | collective-permute-start | bytes 159752 | tf_op jit(solution)/shard_map/ppermute | solution.py:556
  9.4 1.2 %collective-permute-start.4 = (f32[104,128]{1,0:T(8,128)S(1)}, f32[104,128]{1,0:T(8,128)S(1)}, u32[]{:S(2)}, u32[]{:S(2)}) collective-permute-start(f32[104,128]{1,0:T(8,128)S(1)} %collective-permute-done.1.near), channel_id=1, source_target_pairs={{0,2},{1,3},{4,6},{5,7},{8,10},{9,11},{12,14},{13,15},{16,18},{17,... | collective-permute-start | bytes 159752 | tf_op jit(solution)/shard_map/ppermute | solution.py:556
  9.6 1.2 %collective-permute-start.5 = (f32[104,128]{1,0:T(8,128)S(1)}, f32[104,128]{1,0:T(8,128)S(1)}, u32[]{:S(2)}, u32[]{:S(2)}) collective-permute-start(f32[104,128]{1,0:T(8,128)S(1)} %collective-permute-done.2.skip), channel_id=1, source_target_pairs={{0,2},{1,3},{4,6},{5,7},{8,10},{9,11},{12,14},{13,15},{16,18},{17,... | collective-permute-start | bytes 159752 | tf_op jit(solution)/shard_map/ppermute | solution.py:556
  11.1 4.2 %collective-permute-start.6 = (f32[104,128]{1,0:T(8,128)S(1)}, f32[104,128]{1,0:T(8,128)S(1)}, u32[]{:S(2)}, u32[]{:S(2)}) collective-permute-start(f32[104,128]{1,0:T(8,128)S(1)} %get-tuple-element.33.mine), channel_id=1, source_target_pairs={{0,1},{1,0},{2,3},{3,2},{4,5},{5,4},{6,7},{7,6},{8,9},{9,8},{10,11... | collective-permute-start | bytes 159752 | tf_op jit(solution)/shard_map/ppermute | solution.py:556

commit v5 on v4

--- a/solution.py
+++ b/solution.py
@@ -333,40 +333,58 @@
 
 
 def sweep_kernel(
-    sheets, blocks, tiles, own, partner, near, skip, far, near_in, skip_in, out, masks
+    sheets,
+    blocks,
+    tiles,
+    own,
+    partner,
+    near,
+    skip,
+    far,
+    near_in,
+    skip_in,
+    far_in,
+    mine,
+    theirs,
+    masks,
 ):
     n = sheets * blocks
+    edge = 2 * blocks
     tile = lax.axis_index("tile")
     block = lax.axis_index("layer")
-    first = jnp.logical_or(tile == 0, tile == tiles - 1)
-    second = jnp.logical_or(tile == 2, tile == tiles - 3)
-    beside = jnp.logical_or(tile == 1, tile == tiles - 2)
-    keep_outer = jnp.where(first, 0.0, 1.0)
-    keep_far = jnp.where(jnp.logical_or(first, second), 0.0, 1.0)
-    keep_inner = jnp.where(beside, 0.0, 1.0)
-
-    def load(ref, start, rows, keep=None):
-        value = ref[start : start + rows, :]
-        return value if keep is None else keep * value
-
-    def window(start, rows):
-        return [
-            load(skip_in, start, rows, keep_outer),
-            load(near, start, rows, keep_outer),
-            load(own, start, rows),
-            load(partner, start, rows),
-            load(near_in, start, rows, keep_inner),
+    other = tile + 1 - 2 * lax.rem(tile, 2)
+
+    def ends(t):
+        return jnp.logical_or(t == 0, t == tiles - 1)
+
+    def near_ends(t):
+        return jnp.logical_or(ends(t), jnp.logical_or(t == 2, t == tiles - 3))
+
+    keep = [jnp.where(test(t), 0.0, 1.0) for t in (tile, other) for test in (ends, near_ends)]
+
+    def window(start, rows, width):
+        rows = slice(start, start + rows)
+        values = [
+            keep[1] * far[rows, :] if width == 8 else None,
+            keep[0] * skip_in[rows, :],
+            keep[0] * near[rows, :],
+            own[rows, :],
+            partner[rows, :],
+            keep[2] * near_in[rows, :],
+            keep[2] * skip[rows, :],
+            keep[3] * far_in[rows, :] if width == 8 else None,
         ]
-
-    warmth = [load(far, 0, n, keep_far)] + window(0, n) + [load(skip, 0, n, keep_inner)]
-    volt = [load(far, n, n, keep_far)] + window(n, n) + [load(skip, n, n, keep_inner)]
-    slope = window(2 * n, n)
-    free = window(3 * n, 2 * blocks)
+        return [value for value in values if value is not None]
+
+    warmth = window(0, n, 8)
+    volt = window(n, n, 8)
+    slope = window(2 * n, n, 6)
+    free = window(3 * n, edge, 6)
     for i in range(5):
-        masks[2 * i * blocks : 2 * (i + 1) * blocks, :] = free[i]
-    free = [jnp.concatenate([m] * (n // m.shape[0]), axis=0) for m in free]
+        masks[i * edge : (i + 1) * edge, :] = free[i]
+    free = [jnp.concatenate([m] * (n // edge), axis=0) for m in free]
     temp = []
-    for i in range(5):
+    for i in range(6):
         w = warmth[i + 1]
         around = warmth[i] + warmth[i + 2] + along_sheets(w, blocks) + along_span(w, blocks)
         temp.append(w + slope[i] * (around - 6.0 * w))
@@ -381,13 +399,22 @@
             )
             for i in range(len(volt) - 2)
         ]
-    out[0:n, :] = temp[2]
-    out[n : 2 * n, :] = volt[0]
-    for i in range(5):
-        for k, value in enumerate((warmth[i + 1], slope[i])):
-            edge = jnp.where(block == 0, value[n - blocks :, :], value[0:blocks, :])
-            start = 2 * n + (2 * i + k) * blocks
-            out[start : start + blocks, :] = edge
+    edges = [
+        jnp.concatenate(
+            [
+                jnp.where(block == 0, value[n - blocks :, :], value[0:blocks, :])
+                for value in (warmth[i + 1], slope[i])
+            ],
+            axis=0,
+        )
+        for i in range(6)
+    ]
+    for out, order in ((mine, range(5)), (theirs, range(5, 0, -1))):
+        side = 0 if out is mine else 1
+        out[0:n, :] = temp[2 + side]
+        out[n : 2 * n, :] = volt[side]
+        for i, at in enumerate(order):
+            out[2 * n + i * edge : 2 * n + (i + 1) * edge, :] = edges[at]
 
 
 def react(surface_base, gain, rate, node_voltage):
@@ -563,6 +590,7 @@
     skipping = both_layers(mutual([(t, t + 3) for t in range(0, tiles - 3, 2)]))
     skipping = skipping + across([1, tiles - 2])
     layers = across(range(tiles))
+    crossed = [(t * 2 + j, (t ^ 1) * 2 + 1 - j) for t in range(tiles) for j in range(2)]
 
     own = call(
         functools.partial(pack_kernel, blocks),
@@ -624,16 +652,21 @@
     near_in = send(near, cores)
     near, skip, far, held, local = lax.optimization_barrier((near, skip, far, held, local))
     skip_in = send(skip, cores)
-    mine, masks = call(
+    far_in = send(far, cores)
+    mine, theirs, masks = call(
         functools.partial(sweep_kernel, sheets, blocks, tiles),
         "sweeps",
-        (shaped(2 * n + 5 * edge, LANES), shaped(5 * edge, LANES)),
-        [VMEM] * 7,
-        (VMEM, VMEM),
+        (
+            shaped(2 * n + 5 * edge, LANES),
+            shaped(2 * n + 5 * edge, LANES),
+            shaped(5 * edge, LANES),
+        ),
+        [VMEM] * 8,
+        (VMEM,) * 3,
         10**6,
         500000,
-    )(own, partner, near, skip, far, near_in, skip_in)
-    other = send(mine, layers)
+    )(own, partner, near, skip, far, near_in, skip_in, far_in)
+    other = send(theirs, crossed)
     masks, turned = lax.optimization_barrier((masks, sheet_node_link_matrix.T))
     link, turned = call(
         functools.partial(link_kernel, blocks, 2),

time: 17.3 us -> 17.3 us (level)
    ppermute x8 -> x9, starting transfers between devices: 7.59 us -> 7.52 us  [send(): return lax.ppermute(value, ('tile', 'layer'), pairs)]
    ppermute x8 -> x9, waiting for transfers between devices: 2.11 us -> 2.15 us  [send(): return lax.ppermute(value, ('tile', 'layer'), pairs)]
  transfers between devices with their start and end apart: 8 -> 9, of which waited for: 5 -> 4; matrix products, arithmetic and copies ran while one was open for 0% -> 0% of each run, Pallas kernels for 23% -> 24%
where the time goes in v5:
time: 17.3 us; the launch traced here: 17.1 us
  starting transfers between devices  7.52 us (43%)
  Pallas kernels  6.68 us (39%)
  waiting for transfers between devices  2.15 us (12%)
  between operations  0.71 us (4%)
    ppermute x9, starting transfers between devices, send(): return lax.ppermute(value, ('tile', 'layer'), pairs)  7.52 us
    ppermute x9, waiting for transfers between devices, send(): return lax.ppermute(value, ('tile', 'layer'), pairs)  2.15 us
    pallas_call x1, Pallas kernels, per_device(): call(functools.partial(reaction_kernel, sheets, blocks), 'reaction', (sha...  1.77 us
    pallas_call x1, Pallas kernels, per_device(): call(grain_kernel, 'grains', shaped(shells, nodes, LANES), [VMEM] * 2, VM...  1.55 us
    pallas_call x1, Pallas kernels, per_device(): call(local_kernel, 'columns', (shaped(shells, nodes, LANES), shaped(2 * n...  1.4 us
    pallas_call x1, Pallas kernels, per_device(): call(functools.partial(pack_kernel, blocks), 'pack', shaped(3 * n + edge,...  0.86 us
    pallas_call x1, Pallas kernels, per_device(): call(functools.partial(link_kernel, blocks, 2), 'links', (shaped(points *...  0.8 us
  transfers between devices with their start and end apart: 9, of which 4 were waited for; matrix products, arithmetic and copies ran while one was open for 0% of the time, Pallas kernels for 24%

profile of v5, /device:TPU:0, one launch (start us, length us, event | category | flops | bytes accessed | tf_op | source)
XLA Modules:
  0.0 17.1 jit_solution(8155621106800709467)
XLA Ops:
  0.6 0.0 copy-start
  0.6 0.0 copy-start.1
  0.7 0.9 %pack.1.own = f32[104,128]{1,0:T(8,128)S(1)} custom-call(f32[4]{0:T(128)} %storage.1, f32[32,128]{1,0:T(8,128)} %bitcast.16, f32[32,128]{1,0:T(8,128)} %bitcast.17, s32[32,128]{1,0:T(8,128)} %bitcast.18, f32[32,128]{1,0:T(8,128)} %bitcast.19, s32[4,128]{1,0:T(4,128)} %bitcast.20), custom_call_target="tpu_custom_call" | custom-call | flops 1000 | bytes 100000 | tf_op jit(solution)/shard_map/pack/pallas_call | solution.py:595
  1.5 2.5 %collective-permute-start.2 = (f32[104,128]{1,0:T(8,128)S(1)}, f32[104,128]{1,0:T(8,128)S(1)}, u32[]{:S(2)}, u32[]{:S(2)}) collective-permute-start(f32[104,128]{1,0:T(8,128)S(1)} %pack.1.own), channel_id=1, source_target_pairs={{0,6},{1,7},{4,10},{5,11},{8,14},{9,15},{12,18},{13,19},{16,22},{1... | collective-permute-start | bytes 159752 | tf_op jit(solution)/shard_map/ppermute | solution.py:583
  4.0 1.5 %collective-permute-start.1 = (f32[104,128]{1,0:T(8,128)S(1)}, f32[104,128]{1,0:T(8,128)S(1)}, u32[]{:S(2)}, u32[]{:S(2)}) collective-permute-start(f32[104,128]{1,0:T(8,128)S(1)} %pack.1.own), channel_id=1, source_target_pairs={{4,2},{5,3},{8,6},{9,7},{12,10},{13,11},{16,14},{17,15},{20,18},{2... | collective-permute-start | bytes 159752 | tf_op jit(solution)/shard_map/ppermute | solution.py:583
  5.5 0.5 %collective-permute-start.3 = (f32[64,128]{1,0:T(8,128)S(1)}, f32[64,128]{1,0:T(8,128)S(1)}, u32[]{:S(2)}, u32[]{:S(2)}) collective-permute-start(f32[64,128]{1,0:T(8,128)S(1)} %slice.4), channel_id=1, source_target_pairs={{8,2},{9,3},{12,6},{13,7},{16,10},{17,11},{20,14},{21,15},{24,18},... | collective-permute-start | bytes 98312 | tf_op jit(solution)/shard_map/ppermute | solution.py:583
  6.0 1.4 %columns.1 = (f32[32,80,128]{2,1,0:T(8,128)S(1)}, f32[160,128]{1,0:T(8,128)S(1)}, f32[32,128]{1,0:T(8,128)S(1)}) custom-call(f32[32,32]{1,0:T(8,128)} %weights.1, f32[32,80,128]{2,1,0:T(8,128)} %bitcast.14, f32[80,128]{1,0:T(8,128)} %bitcast.15, f32[40,40]{1,0:T(8,128)} %salt_matrix.1), custom_call_target="tpu_custom_call" | custom-call | flops 10000000 | bytes 3000000 | tf_op jit(solution)/shard_map/columns/pallas_call | solution.py:624
  7.4 1.6 %collective-permute-start.8 = (f32[160,128]{1,0:T(8,128)S(1)}, f32[160,128]{1,0:T(8,128)S(1)}, u32[]{:S(2)}, u32[]{:S(2)}) collective-permute-start(f32[160,128]{1,0:T(8,128)S(1)} %get-tuple-element.36.local), channel_id=1, source_target_pairs={{0,1},{1,0},{2,3},{3,2},{4,5},{5,4},{6,7},{7,6},{8,9},{9,8},{10,11... | collective-permute-start | bytes 245768 | tf_op jit(solution)/shard_map/ppermute | solution.py:583
  9.0 0.1 collective-permute-start
  9.1 0.4 %collective-permute-done.3.far = f32[64,128]{1,0:T(8,128)S(1)} collective-permute-done((f32[64,128]{1,0:T(8,128)S(1)}, f32[64,128]{1,0:T(8,128)S(1)}, u32[]{:S(2)}, u32[]{:S(2)}) %collective-permute-start.3) | collective-permute-done | bytes 32800 | tf_op jit(solution)/shard_map/ppermute | solution.py:583
  9.4 0.0 collective-permute-done.2.skip
  9.4 0.0 collective-permute-done.1.near
  9.4 0.2 collective-permute-start.4
  9.6 0.3 %collective-permute-start.5 = (f32[104,128]{1,0:T(8,128)S(1)}, f32[104,128]{1,0:T(8,128)S(1)}, u32[]{:S(2)}, u32[]{:S(2)}) collective-permute-start(f32[104,128]{1,0:T(8,128)S(1)} %collective-permute-done.2.skip), channel_id=1, source_target_pairs={{0,2},{1,3},{4,6},{5,7},{8,10},{9,11},{12,14},{13,15},{16,18},{17,... | collective-permute-start | bytes 159752 | tf_op jit(solution)/shard_map/ppermute | solution.py:583
  9.9 0.2 collective-permute-start.6
  10.1 0.1 collective-permute-done.partner
  10.2 0.9 %collective-permute-done.6.far_in = f32[64,128]{1,0:T(8,128)S(1)} collective-permute-done((f32[64,128]{1,0:T(8,128)S(1)}, f32[64,128]{1,0:T(8,128)S(1)}, u32[]{:S(2)}, u32[]{:S(2)}) %collective-permute-start.6) | collective-permute-done | bytes 32800 | tf_op jit(solution)/shard_map/ppermute | solution.py:583
  11.1 0.0 collective-permute-done.4.near_in
  11.1 0.0 collective-permute-done.5.skip_in
  11.1 0.3 %sweeps.1 = (f32[104,128]{1,0:T(8,128)S(1)}, f32[104,128]{1,0:T(8,128)S(1)}, f32[40,128]{1,0:T(8,128)S(1)}) custom-call(f32[104,128]{1,0:T(8,128)S(1)} %pack.1.own, f32[104,128]{1,0:T(8,128)S(1)} %collective-permute-done.partner, f32[104,128]{1,0:T(8,128)S(1)} %collective-permute-done.1.near, f32[104,128]{1,0:T(8,128)S(1)} %collective-permute-done.2.skip, ...), custom_call_target="tpu_custom_call" | custom-call | flops 1000000 | bytes 500000 | tf_op jit(solution)/shard_map/sweeps/pallas_call | solution.py:656
  11.4 0.7 %collective-permute-start.7 = (f32[104,128]{1,0:T(8,128)S(1)}, f32[104,128]{1,0:T(8,128)S(1)}, u32[]{:S(2)}, u32[]{:S(2)}) collective-permute-start(f32[104,128]{1,0:T(8,128)S(1)} %get-tuple-element.35), channel_id=1, source_target_pairs={{0,3},{1,2},{2,1},{3,0},{4,7},{5,6},{6,5},{7,4},{8,11},{9,10},{10,... | collective-permute-start | bytes 159752 | tf_op jit(solution)/shard_map/ppermute | solution.py:583
  12.2 0.0 collective-permute-done.8.other_local
  12.2 0.0 copy-done.1
  12.2 0.8 %links.1 = (f32[160,64]{1,0:T(8,128)S(1)}, f32[32,160]{1,0:T(8,128)S(1)}) custom-call(f32[16,40]{1,0:T(8,128)S(1)} %bitcast.13), custom_call_target="tpu_custom_call" | custom-call | flops 1000000 | bytes 100000 | tf_op jit(solution)/shard_map/links/pallas_call | solution.py:671
  13.0 0.0 copy-done
  13.0 1.5 %grains.1.base = f32[32,80,128]{2,1,0:T(8,128)S(1)} custom-call(f32[32,80,128]{2,1,0:T(8,128)S(1)} %get-tuple-element.42.grain, f32[32,32]{1,0:T(8,128)S(1)} %copy-done), custom_call_target="tpu_custom_call" | custom-call | flops 1000000000 | bytes 3000000 | tf_op jit(solution)/shard_map/grains/pallas_call | solution.py:681
  14.6 0.7 %collective-permute-done.7.other = f32[104,128]{1,0:T(8,128)S(1)} collective-permute-done((f32[104,128]{1,0:T(8,128)S(1)}, f32[104,128]{1,0:T(8,128)S(1)}, u32[]{:S(2)}, u32[]{:S(2)}) %collective-permute-start.7) | collective-permute-done | bytes 53280 | tf_op jit(solution)/shard_map/ppermute | solution.py:583
  15.3 1.8 %reaction.1 = (f32[32,128]{1,0:T(8,128)}, f32[32,128]{1,0:T(8,128)}, f32[32,128]{1,0:T(8,128)}, f32[32,80,128]{2,1,0:T(8,128)}, f32[80,128]{1,0:T(8,128)}) custom-call(f32[32,128]{1,0:T(8,128)S(1)} %get-tuple-element.28.factors, f32[104,128]{1,0:T(8,128)S(1)} %get-tuple-element.34.mine, f32[104,128]{1,0:T(8,128)S(1)} %collective-permute-done.7.other, ...), custom_call_target="tpu_custom_call" | custom-call | flops 10000000 | bytes 3000000 | tf_op jit(solution)/shard_map/reaction/pallas_call | solution.py:684
  (1 shorter events, 0.0 us)
Async XLA Ops:
  0.6 12.4 %copy-start = (f32[32,32]{1,0:T(8,128)S(1)}, f32[32,32]{1,0:T(8,128)}, u32[]{:S(2)}) copy-start(f32[32,32]{1,0:T(8,128)} %weights.1) | copy-start | bytes 12292
  0.6 11.5 %copy-start.1 = (f32[40,16]{0,1:T(8,128)S(1)}, f32[40,16]{0,1:T(8,128)}, u32[]{:S(2)}) copy-start(f32[40,16]{0,1:T(8,128)} %param.17) | copy-start | bytes 7684
  1.5 7.9 %collective-permute-start.2 = (f32[104,128]{1,0:T(8,128)S(1)}, f32[104,128]{1,0:T(8,128)S(1)}, u32[]{:S(2)}, u32[]{:S(2)}) collective-permute-start(f32[104,128]{1,0:T(8,128)S(1)} %pack.1.own), channel_id=1, source_target_pairs={{0,6},{1,7},{4,10},{5,11},{8,14},{9,15},{12,18},{13,19},{16,22},{1... | collective-permute-start | bytes 159752 | tf_op jit(solution)/shard_map/ppermute | solution.py:583
  4.0 5.4 %collective-permute-start.1 = (f32[104,128]{1,0:T(8,128)S(1)}, f32[104,128]{1,0:T(8,128)S(1)}, u32[]{:S(2)}, u32[]{:S(2)}) collective-permute-start(f32[104,128]{1,0:T(8,128)S(1)} %pack.1.own), channel_id=1, source_target_pairs={{4,2},{5,3},{8,6},{9,7},{12,10},{13,11},{16,14},{17,15},{20,18},{2... | collective-permute-start | bytes 159752 | tf_op jit(solution)/shard_map/ppermute | solution.py:583
  5.5 3.9 %collective-permute-start.3 = (f32[64,128]{1,0:T(8,128)S(1)}, f32[64,128]{1,0:T(8,128)S(1)}, u32[]{:S(2)}, u32[]{:S(2)}) collective-permute-start(f32[64,128]{1,0:T(8,128)S(1)} %slice.4), channel_id=1, source_target_pairs={{8,2},{9,3},{12,6},{13,7},{16,10},{17,11},{20,14},{21,15},{24,18},... | collective-permute-start | bytes 98312 | tf_op jit(solution)/shard_map/ppermute | solution.py:583
  7.4 4.7 %collective-permute-start.8 = (f32[160,128]{1,0:T(8,128)S(1)}, f32[160,128]{1,0:T(8,128)S(1)}, u32[]{:S(2)}, u32[]{:S(2)}) collective-permute-start(f32[160,128]{1,0:T(8,128)S(1)} %get-tuple-element.36.local), channel_id=1, source_target_pairs={{0,1},{1,0},{2,3},{3,2},{4,5},{5,4},{6,7},{7,6},{8,9},{9,8},{10,11... | collective-permute-start | bytes 245768 | tf_op jit(solution)/shard_map/ppermute | solution.py:583
  9.0 1.2 %collective-permute-start = (f32[104,128]{1,0:T(8,128)S(1)}, f32[104,128]{1,0:T(8,128)S(1)}, u32[]{:S(2)}, u32[]{:S(2)}) collective-permute-start(f32[104,128]{1,0:T(8,128)S(1)} %pack.1.own), channel_id=1, source_target_pairs={{0,2},{1,3},{4,6},{5,7},{8,10},{9,11},{12,14},{13,15},{16,18},{17,... | collective-permute-start | bytes 159752 | tf_op jit(solution)/shard_map/ppermute | solution.py:583
  9.4 1.7 %collective-permute-start.4 = (f32[104,128]{1,0:T(8,128)S(1)}, f32[104,128]{1,0:T(8,128)S(1)}, u32[]{:S(2)}, u32[]{:S(2)}) collective-permute-start(f32[104,128]{1,0:T(8,128)S(1)} %collective-permute-done.1.near), channel_id=1, source_target_pairs={{0,2},{1,3},{4,6},{5,7},{8,10},{9,11},{12,14},{13,15},{16,18},{17,... | collective-permute-start | bytes 159752 | tf_op jit(solution)/shard_map/ppermute | solution.py:583
  9.6 1.6 %collective-permute-start.5 = (f32[104,128]{1,0:T(8,128)S(1)}, f32[104,128]{1,0:T(8,128)S(1)}, u32[]{:S(2)}, u32[]{:S(2)}) collective-permute-start(f32[104,128]{1,0:T(8,128)S(1)} %collective-permute-done.2.skip), channel_id=1, source_target_pairs={{0,2},{1,3},{4,6},{5,7},{8,10},{9,11},{12,14},{13,15},{16,18},{17,... | collective-permute-start | bytes 159752 | tf_op jit(solution)/shard_map/ppermute | solution.py:583
  9.9 1.2 %collective-permute-start.6 = (f32[64,128]{1,0:T(8,128)S(1)}, f32[64,128]{1,0:T(8,128)S(1)}, u32[]{:S(2)}, u32[]{:S(2)}) collective-permute-start(f32[64,128]{1,0:T(8,128)S(1)} %collective-permute-done.3.far), channel_id=1, source_target_pairs={{0,2},{1,3},{4,6},{5,7},{8,10},{9,11},{12,14},{13,15},{16,18},{17,... | collective-permute-start | bytes 98312 | tf_op jit(solution)/shard_map/ppermute | solution.py:583
  11.4 3.8 %collective-permute-start.7 = (f32[104,128]{1,0:T(8,128)S(1)}, f32[104,128]{1,0:T(8,128)S(1)}, u32[]{:S(2)}, u32[]{:S(2)}) collective-permute-start(f32[104,128]{1,0:T(8,128)S(1)} %get-tuple-element.35), channel_id=1, source_target_pairs={{0,3},{1,2},{2,1},{3,0},{4,7},{5,6},{6,5},{7,4},{8,11},{9,10},{10,... | collective-permute-start | bytes 159752 | tf_op jit(solution)/shard_map/ppermute | solution.py:583
